TPU v7x, 256 devices: a whole 4x4x8 slice. The times are simulated.
256 devices in a mesh: ctx: 32 (over z, x), head: 8 (over y, core).
Axes of the slice: x: 4, y: 4, z: 8, core: 2. Of those that a mesh axis runs over, the one named last changes fastest.
Arguments:
- query: bfloat16 [32, 2, 128, 8192], P('ctx', None, 'head'), may hold values from -200 to 200
- keyval: bfloat16 [32, 2, 2, 128, 1024], P('ctx', None, None, 'head'), may hold values from -6 to 6
- doc_blocks: int32 [4], replicated, may hold values from 1 to 48, 64 in all
Outputs:
- attended: bfloat16 [32, 2, 128, 8192], P('ctx', None, 'head')
Inputs may be any that keep to these rules, and one draw needn't show every extreme that they name: `doc_blocks`: documents fill the sequence in order; the longest has exactly 48 blocks.
All inputs are finite; a program needn't handle non-finite values.
Results may differ from a plain program's by a relative error of at most 0.0038.
Values may be sent and summed in bfloat16 or wider, within the bound.
No kernel may reach another device: no remote copies, remote signals or barrier semaphores. Data moves between devices by JAX's collectives and lax.ppermute only.
A program may use at most 64 MiB of HBM per device.

v0:
```python
import functools

import jax
import jax.numpy as jnp
from jax import lax
from jax.experimental import pallas as pl
from jax.experimental.pallas import tpu as pltpu
from jax.sharding import Mesh
from jax.sharding import PartitionSpec as P

QUERY_HEADS = 64
KEY_VALUE_HEADS = 8
HEAD_WIDTH = 128
GROUP = QUERY_HEADS // KEY_VALUE_HEADS
BLK = 128
Z, X = 8, 4
SPAN_COUNT = 2 * Z * X
CTX = ("z", "x")
FAR = -1e30
ORDER = (0, 1, 3, 2)
SCALE = HEAD_WIDTH ** (-0.5) * 1.4426950408889634


def attend(steps, count, first, last, docs_ref, rows_ref, *refs):
    sent, refs = refs[:count], refs[count:]
    if not first:
        old, refs = refs[:3], refs[3:]
    if last:
        out_ref, refs = refs[0], refs[1:]
    max_ref, sum_ref, acc_ref = refs[:3]
    if first:
        sent_ref, rows_ref = rows_ref, refs[3]
        tokens = sent_ref.shape[2]
        for src in range(sent_ref.shape[0]):
            for g in range(GROUP):
                for half in range(2):
                    rows_ref[half, g, src * tokens : (src + 1) * tokens] = sent_ref[src, 2 * g + half]
        max_ref[...] = jnp.full_like(max_ref, FAR)
        sum_ref[...] = jnp.zeros_like(sum_ref)
        acc_ref[...] = jnp.zeros_like(acc_ref)
    elif last:
        for ref, kept in zip(refs[:3], old):
            ref[...] = kept[...]
    tilt = lax.broadcasted_iota(jnp.int32, (BLK, BLK), 1) - lax.broadcasted_iota(
        jnp.int32, (BLK, BLK), 0
    )
    my_z, x_index = lax.axis_index("z"), lax.axis_index("x")
    place = my_z * X + x_index
    owns = (place, SPAN_COUNT - 1 - place)
    starts = [jnp.int32(0), jnp.int32(0)]
    end = jnp.int32(0)
    for j in range(docs_ref.shape[0]):
        end = end + docs_ref[j]
        starts = [jnp.where(end <= own, end, start) for own, start in zip(owns, starts)]

    for away, picks in steps:
        blocks = [sent[array].at[i] for array, i in picks]
        z_index = lax.rem(my_z + away + Z, Z)

        def pair(step, _, blocks=blocks, z_index=z_index):
            half, side = step // 2, step % 2
            start = jnp.where(half == 0, starts[0], starts[1])
            own = jnp.where(half == 0, owns[0], owns[1])
            low = jnp.where(side == 0, z_index * X, SPAN_COUNT - X - z_index * X)

            def fold(masked):
                keys = jnp.concatenate([ref[side] for ref in blocks], axis=0)
                values = jnp.concatenate([ref[2 + side] for ref in blocks], axis=0)
                rows = rows_ref[half].reshape(GROUP * BLK, HEAD_WIDTH)
                scores = (
                    lax.dot_general(
                        rows, keys, (((1,), (1,)), ((), ())), preferred_element_type=jnp.float32
                    )
                    * SCALE
                )
                parts = [
                    scores[:, d * BLK : (d + 1) * BLK].reshape(GROUP, BLK, BLK) for d in range(X)
                ]
                if masked:
                    for d in range(X):
                        place = lax.rem(x_index - ORDER[d] + X, X)
                        span = low + jnp.where(side == 0, place, X - 1 - place)
                        reach = jnp.where(span >= start, (own - span) * BLK, -2 * BLK)
                        parts[d] = jnp.where((tilt <= reach)[None], parts[d], 2 * FAR)
                top = functools.reduce(jnp.maximum, parts)
                before = max_ref[half]
                now = jnp.maximum(before, jnp.max(top, axis=2, keepdims=True))
                fade = jnp.exp2(before - now)
                parts = [jnp.exp2(part - now) for part in parts]
                max_ref[half] = now
                sum_ref[half] = sum_ref[half] * fade + functools.reduce(jnp.add, parts)
                weights = jnp.concatenate([part.astype(jnp.bfloat16) for part in parts], axis=2)
                added = jnp.dot(
                    weights.reshape(GROUP * BLK, X * BLK), values, preferred_element_type=jnp.float32
                )
                acc_ref[half] = acc_ref[half] * fade + added.reshape(GROUP, BLK, HEAD_WIDTH)

            touched = (low <= own) & (low + X > start)
            whole = (low + X <= own) & (low >= start)
            pl.when(whole)(lambda: fold(False))
            pl.when(touched & jnp.logical_not(whole))(lambda: fold(True))
            return 0

        lax.fori_loop(0, 4, pair, 0)

    if last:
        tokens = out_ref.shape[2]
        for half in range(2):
            for g in range(GROUP):
                totals = jnp.sum(sum_ref[half, g], axis=1, keepdims=True)
                result = (acc_ref[half, g] / totals).astype(jnp.bfloat16)
                for src in range(out_ref.shape[0]):
                    out_ref[src, half, :, g * HEAD_WIDTH : (g + 1) * HEAD_WIDTH] = result[
                        src * tokens : (src + 1) * tokens
                    ]


def run(doc_blocks, query, steps, bundles, state, last, shape=None):
    first = state is None
    state_shape = (2, GROUP, BLK, HEAD_WIDTH)
    vmem = pl.BlockSpec(memory_space=pltpu.VMEM)
    kept = [] if first else list(state)
    refs = len(bundles)
    if last:
        out_shape = jax.ShapeDtypeStruct(shape, jnp.bfloat16)
        out_specs, scratch, aliases = vmem, [pltpu.VMEM(state_shape, jnp.float32)] * 3, {}
    else:
        out_shape = [jax.ShapeDtypeStruct(state_shape, jnp.float32)] * 3
        if first:
            out_shape.append(jax.ShapeDtypeStruct(state_shape, jnp.bfloat16))
        out_specs, scratch = [vmem] * len(out_shape), []
        aliases = {} if first else {2 + refs + i: i for i in range(3)}
    pairs = 4 * len(steps)
    return pl.pallas_call(
        functools.partial(attend, steps, refs, first, last),
        out_shape=out_shape,
        in_specs=[pl.BlockSpec(memory_space=pltpu.SMEM)] + [vmem] * (1 + refs + len(kept)),
        out_specs=out_specs,
        scratch_shapes=scratch,
        input_output_aliases=aliases,
        compiler_params=pltpu.CompilerParams(vmem_limit_bytes=20 * 2**20),
        cost_estimate=pl.CostEstimate(
            flops=pairs * 4 * 1024 * 512 * 128, bytes_accessed=2**22, transcendentals=pairs * 2**19
        ),
    )(doc_blocks, query, *bundles, *kept)


def moved(moves, operands, shapes):
    left = pl.BlockSpec(memory_space=pl.ANY)

    def body(*refs):
        ins, outs, sem = refs[: len(operands)], refs[len(operands) : -1], refs[-1]
        copies = [
            pltpu.make_async_copy(ins[i].at[src], outs[o].at[dst], sem.at[n])
            for n, (i, src, o, dst) in enumerate(moves)
        ]
        for copy in copies:
            copy.start()
        for copy in copies:
            copy.wait()

    return pl.pallas_call(
        body,
        out_shape=[jax.ShapeDtypeStruct(shape, jnp.bfloat16) for shape in shapes],
        in_specs=[left] * len(operands),
        out_specs=[left] * len(shapes),
        scratch_shapes=[pltpu.SemaphoreType.DMA((len(moves),))],
        compiler_params=pltpu.CompilerParams(vmem_limit_bytes=2**20),
        cost_estimate=pl.CostEstimate(flops=0, bytes_accessed=2**20, transcendentals=0),
    )(*operands)


def pack(in_ref, out_ref):
    heads, parts, _, width = out_ref.shape
    lead = in_ref.shape[0]
    for h in range(heads):
        for part in range(parts):
            at = (h * (parts // lead) + part // lead) * width
            out_ref[h, part] = in_ref[part % lead, :, at : at + width]


def unpack(in_ref, out_ref):
    tokens = in_ref.shape[2]
    for src in range(in_ref.shape[0]):
        for j in range(in_ref.shape[1]):
            out_ref[0, j, src * tokens : (src + 1) * tokens] = in_ref[src, j]


def arranged(body, operands, shapes):
    vmem = pl.BlockSpec(memory_space=pltpu.VMEM)
    return pl.pallas_call(
        body,
        out_shape=[jax.ShapeDtypeStruct(shape, jnp.bfloat16) for shape in shapes],
        in_specs=[vmem] * len(operands),
        out_specs=[vmem] * len(shapes),
        compiler_params=pltpu.CompilerParams(vmem_limit_bytes=8 * 2**20),
        cost_estimate=pl.CostEstimate(flops=0, bytes_accessed=2**20, transcendentals=0),
    )(*operands)


def shift(x, axis, size, by):
    return lax.ppermute(x, axis, [(i, (i + by) % size) for i in range(size)])


def exchange(x):
    return lax.all_to_all(x, "head", split_axis=0, concat_axis=0, tiled=True)


def local(query, keyval, doc_blocks):
    tokens = keyval.shape[3]
    wide = GROUP * HEAD_WIDTH
    every = slice(None)
    heads = KEY_VALUE_HEADS
    kv = keyval.reshape(4, tokens, heads * HEAD_WIDTH)
    [kv] = arranged(pack, [kv], [(heads, 4, tokens, HEAD_WIDTH)])
    [near] = arranged(unpack, [exchange(kv)], [(1, 4, BLK, HEAD_WIDTH)])
    q = query.reshape(2, tokens, heads * wide)
    [q] = arranged(pack, [q], [(heads, 2 * GROUP, tokens, HEAD_WIDTH)])
    q = exchange(q)
    shape = (heads, 2, tokens, wide)
    beside = [shift(near, "x", X, d) for d in ORDER[1:3]]
    far = shift(near, "x", X, ORDER[3])
    block = near.shape[1:]
    [trio] = moved([(i, 0, 0, i) for i in range(3)], [near, *beside], [(3, *block)])

    picks = [(0, 0), (0, 1), (0, 2), (1, 0)]
    *state, q = run(doc_blocks, q, [(0, picks)], [trio, far], None, False)
    up = down = trio
    for k in range(1, Z // 2):
        up, down = shift(up, "z", Z, 1), shift(down, "z", Z, -1)
        both = [(0, 2, 0, 0), (1, 2, 0, 1)]
        if k < Z // 2 - 1:
            [cross] = moved(both, [up, down], [(2, *block)])
        else:
            cross, pair, lone = moved(
                [*both, (0, pl.ds(0, 2), 1, every), (1, 2, 2, 0)],
                [up, down],
                [(2, *block), (2, *block), (1, *block)],
            )
        cross = shift(cross, "x", X, -1)
        picks = [[(side, 0), (side, 1), (side, 2), (2, side)] for side in range(2)]
        steps = [(-k, picks[0]), (k, picks[1])]
        if k > 1:
            (up, down), state = lax.optimization_barrier(((up, down), state))
        state = run(doc_blocks, q, steps, [up, down, cross], state, False)
    pair, lone = shift(pair, "z", Z, 1), shift(lone, "z", Z, -1)
    cross = shift(lone, "x", X, -1)
    picks = [(0, 0), (0, 1), (1, 0), (2, 0)]
    out = run(doc_blocks, q, [(-(Z // 2), picks)], [pair, lone, cross], state, True, shape)

    out = exchange(out)
    [out] = moved(
        [(0, h, 0, (every, every, pl.ds(h * wide, wide))) for h in range(KEY_VALUE_HEADS)],
        [out],
        [(2, tokens, KEY_VALUE_HEADS * wide)],
    )
    return out.reshape(query.shape)


def solution(mesh):
    torus = Mesh(mesh.devices.reshape(Z, X, mesh.shape["head"]), ("z", "x", "head"))
    placed = (P(CTX, None, "head", None), P(CTX, None, None, "head", None), P())
    return jax.shard_map(
        local, mesh=torus, in_specs=placed, out_specs=P(CTX, None, "head", None), check_vma=False
    )
```

profile of v0, /device:TPU:1, one launch (start us, length us, event | category | flops | bytes accessed | tf_op | source)
XLA Modules:
  0.0 91.7 jit_solution(11716291335408550379)
XLA Ops:
  0.0 0.9 copy-done.1
  0.9 11.0 %all_to_all.15.in_ref = bf16[8,4,16,128]{3,2,1,0:T(8,128)(2,1)S(1)} all-to-all(bf16[8,4,16,128]{3,2,1,0:T(8,128)(2,1)S(1)} %shard_map.38), channel_id=1, replica_groups=mesh['z'=8,'x'=4,'head'=8] {'head'}, dimensions={0} | all-to-all | bytes 262144 | tf_op jit(solution)/shard_map/all_to_all | solution.py:206
  12.0 1.3 %collective-permute-start = (bf16[1,4,128,128]{3,2,1,0:T(8,128)(2,1)S(1)}, bf16[1,4,128,128]{3,2,1,0:T(8,128)(2,1)S(1)}, u32[]{:S(2)}, u32[]{:S(2)}) collective-permute-start(bf16[1,4,128,128]{3,2,1,0:T(8,128)(2,1)S(1)} %shard_map.39.refs_0_), channel_id=1, source_target_pairs={{0,8},{8,16},{16,24},{24,0},{1,9},{9,17},{17,25},{25,1},{2,10},{10... | collective-permute-start | bytes 393224 | tf_op jit(solution)/shard_map/ppermute | solution.py:202
  13.3 1.5 %collective-permute-start.1 = (bf16[1,4,128,128]{3,2,1,0:T(8,128)(2,1)S(1)}, bf16[1,4,128,128]{3,2,1,0:T(8,128)(2,1)S(1)}, u32[]{:S(2)}, u32[]{:S(2)}) collective-permute-start(bf16[1,4,128,128]{3,2,1,0:T(8,128)(2,1)S(1)} %shard_map.39.refs_0_), channel_id=1, source_target_pairs={{0,24},{8,0},{16,8},{24,16},{1,25},{9,1},{17,9},{25,17},{2,26},{10... | collective-permute-start | bytes 393224 | tf_op jit(solution)/shard_map/ppermute | solution.py:202
  14.7 2.7 %collective-permute-done.refs_1_ = bf16[1,4,128,128]{3,2,1,0:T(8,128)(2,1)S(1)} collective-permute-done((bf16[1,4,128,128]{3,2,1,0:T(8,128)(2,1)S(1)}, bf16[1,4,128,128]{3,2,1,0:T(8,128)(2,1)S(1)}, u32[]{:S(2)}, u32[]{:S(2)}) %collective-permute-start) | collective-permute-done | bytes 131104 | tf_op jit(solution)/shard_map/ppermute | solution.py:202
  17.4 0.0 collective-permute-done.1.refs_2_
  17.4 0.5 shard_map.40.refs_0_
  18.0 1.7 %collective-permute-start.3 = (bf16[3,4,128,128]{3,2,1,0:T(8,128)(2,1)S(1)}, bf16[3,4,128,128]{3,2,1,0:T(8,128)(2,1)S(1)}, u32[]{:S(2)}, u32[]{:S(2)}) collective-permute-start(bf16[3,4,128,128]{3,2,1,0:T(8,128)(2,1)S(1)} %shard_map.40.refs_0_), channel_id=1, source_target_pairs={{0,32},{32,64},{64,96},{96,128},{128,160},{160,192},{192,224},{224... | collective-permute-start | bytes 1179656 | tf_op jit(solution)/shard_map/ppermute | solution.py:202
  19.7 4.0 %collective-permute-start.5 = (bf16[3,4,128,128]{3,2,1,0:T(8,128)(2,1)S(1)}, bf16[3,4,128,128]{3,2,1,0:T(8,128)(2,1)S(1)}, u32[]{:S(2)}, u32[]{:S(2)}) collective-permute-start(bf16[3,4,128,128]{3,2,1,0:T(8,128)(2,1)S(1)} %shard_map.40.refs_0_), channel_id=1, source_target_pairs={{0,224},{32,0},{64,32},{96,64},{128,96},{160,128},{192,160},{224,1... | collective-permute-start | bytes 1179656 | tf_op jit(solution)/shard_map/ppermute | solution.py:202
  23.7 0.0 copy-done
  23.7 0.9 shard_map.37
  24.6 5.6 %all-to-all-start = ((bf16[8,16,16,128]{3,2,1,0:T(8,128)(2,1)}), bf16[8,16,16,128]{3,2,1,0:T(8,128)(2,1)S(1)}, u32[]{:S(2)}, u32[]{:S(2)}) async-start(bf16[8,16,16,128]{3,2,1,0:T(8,128)(2,1)} %shard_map.37), calls=%async_computation | async-start | bytes 1048576 | tf_op jit(solution)/shard_map/all_to_all | solution.py:206
  30.2 0.9 collective-permute-done.3.refs_0_
  31.1 0.0 collective-permute-done.5.refs_1_
  31.1 0.3 shard_map.42
  31.4 2.1 %collective-permute-start.7 = (bf16[2,4,128,128]{3,2,1,0:T(8,128)(2,1)S(1)}, bf16[2,4,128,128]{3,2,1,0:T(8,128)(2,1)S(1)}, u32[]{:S(2)}, u32[]{:S(2)}) collective-permute-start(bf16[2,4,128,128]{3,2,1,0:T(8,128)(2,1)S(1)} %shard_map.42), channel_id=1, source_target_pairs={{0,24},{8,0},{16,8},{24,16},{1,25},{9,1},{17,9},{25,17},{2,26},{10... | collective-permute-start | bytes 786440 | tf_op jit(solution)/shard_map/ppermute | solution.py:202
  33.5 0.9 collective-permute-start.2
  34.4 0.0 collective-permute-start.4
  34.4 2.7 %collective-permute-start.6 = (bf16[3,4,128,128]{3,2,1,0:T(8,128)(2,1)S(1)}, bf16[3,4,128,128]{3,2,1,0:T(8,128)(2,1)S(1)}, u32[]{:S(2)}, u32[]{:S(2)}) collective-permute-start(bf16[3,4,128,128]{3,2,1,0:T(8,128)(2,1)S(1)} %collective-permute-done.5.refs_1_), channel_id=1, source_target_pairs={{0,224},{32,0},{64,32},{96,64},{128,96},{160,128},{192,160},{224,1... | collective-permute-start | bytes 1179656 | tf_op jit(solution)/shard_map/ppermute | solution.py:202
  37.1 1.7 %collective-permute-done.2.refs_1_ = bf16[1,4,128,128]{3,2,1,0:T(8,128)(2,1)S(1)} collective-permute-done((bf16[1,4,128,128]{3,2,1,0:T(8,128)(2,1)S(1)}, bf16[1,4,128,128]{3,2,1,0:T(8,128)(2,1)S(1)}, u32[]{:S(2)}, u32[]{:S(2)}) %collective-permute-start.2) | collective-permute-done | bytes 131104 | tf_op jit(solution)/shard_map/ppermute | solution.py:202
  38.8 0.9 all-to-all-done.rows_ref
  39.7 0.0 copy-done.2
  39.7 3.0 %shard_map.41 = (f32[2,8,128,128]{3,2,1,0:T(8,128)S(1)}, f32[2,8,128,128]{3,2,1,0:T(8,128)S(1)}, f32[2,8,128,128]{3,2,1,0:T(8,128)S(1)}, bf16[2,8,128,128]{3,2,1,0:T(8,128)(2,1)S(1)}) custom-call(s32[4]{0:T(128)S(1)} %copy-done.2, bf16[8,16,16,128]{3,2,1,0:T(8,128)(2,1)S(1)} %all-to-all-done.rows_ref, bf16[3,4,128,128]{3,2,1,0:T(8,128)(2,1)S(1)} %shard_map.40.refs_0_, ...), custom_call_target="tpu_custom_call" | custom-call | flops 1073741824 | bytes 4194304 | tf_op jit(solution)/shard_map/pallas_call | solution.py:134
  42.7 0.0 collective-permute-done.7.refs_2_
  42.7 3.7 %shard_map.43 = (f32[2,8,128,128]{3,2,1,0:T(8,128)S(1)}, f32[2,8,128,128]{3,2,1,0:T(8,128)S(1)}, f32[2,8,128,128]{3,2,1,0:T(8,128)S(1)}) custom-call(s32[4]{0:T(128)S(1)} %copy-done.2, bf16[2,8,128,128]{3,2,1,0:T(8,128)(2,1)S(1)} %get-tuple-element.31.rows_ref, ...), custom_call_target="tpu_custom_call", output_to_operand_aliasing={{0}: (5, {}), {1}: (6, {}), {2}: (7, {})} | custom-call | flops 2147483648 | bytes 4194304 | tf_op jit(solution)/shard_map/pallas_call | solution.py:134
  46.4 0.0 collective-permute-done.4.refs_0_
  46.4 0.0 collective-permute-done.6.refs_1_
  46.4 0.1 collective-permute-start.8
  46.5 2.7 %collective-permute-start.9 = (bf16[3,4,128,128]{3,2,1,0:T(8,128)(2,1)S(1)}, bf16[3,4,128,128]{3,2,1,0:T(8,128)(2,1)S(1)}, u32[]{:S(2)}, u32[]{:S(2)}) collective-permute-start(bf16[3,4,128,128]{3,2,1,0:T(8,128)(2,1)S(1)} %collective-permute-done.6.refs_1_), channel_id=1, source_target_pairs={{0,224},{32,0},{64,32},{96,64},{128,96},{160,128},{192,160},{224,1... | collective-permute-start | bytes 1179656 | tf_op jit(solution)/shard_map/ppermute | solution.py:202
  49.2 0.3 shard_map.45
  49.5 2.8 %collective-permute-start.13 = (bf16[2,4,128,128]{3,2,1,0:T(8,128)(2,1)S(1)}, bf16[2,4,128,128]{3,2,1,0:T(8,128)(2,1)S(1)}, u32[]{:S(2)}, u32[]{:S(2)}) collective-permute-start(bf16[2,4,128,128]{3,2,1,0:T(8,128)(2,1)S(1)} %shard_map.45), channel_id=1, source_target_pairs={{0,24},{8,0},{16,8},{24,16},{1,25},{9,1},{17,9},{25,17},{2,26},{10... | collective-permute-start | bytes 786440 | tf_op jit(solution)/shard_map/ppermute | solution.py:202
  52.3 2.6 %collective-permute-done.8.refs_0_ = bf16[3,4,128,128]{3,2,1,0:T(8,128)(2,1)S(1)} collective-permute-done((bf16[3,4,128,128]{3,2,1,0:T(8,128)(2,1)S(1)}, bf16[3,4,128,128]{3,2,1,0:T(8,128)(2,1)S(1)}, u32[]{:S(2)}, u32[]{:S(2)}) %collective-permute-start.8) | collective-permute-done | bytes 393248 | tf_op jit(solution)/shard_map/ppermute | solution.py:202
  54.9 0.0 collective-permute-done.9.refs_1_
  54.9 0.5 shard_map.44
  55.4 3.1 %collective-permute-start.14 = (bf16[2,4,128,128]{3,2,1,0:T(8,128)(2,1)S(1)}, bf16[2,4,128,128]{3,2,1,0:T(8,128)(2,1)S(1)}, u32[]{:S(2)}, u32[]{:S(2)}) collective-permute-start(bf16[2,4,128,128]{3,2,1,0:T(8,128)(2,1)S(1)} %get-tuple-element.50), channel_id=1, source_target_pairs={{0,24},{8,0},{16,8},{24,16},{1,25},{9,1},{17,9},{25,17},{2,26},{10... | collective-permute-start | bytes 786440 | tf_op jit(solution)/shard_map/ppermute | solution.py:202
  58.5 2.4 %collective-permute-start.11 = (bf16[1,4,128,128]{3,2,1,0:T(8,128)(2,1)S(1)}, bf16[1,4,128,128]{3,2,1,0:T(8,128)(2,1)S(1)}, u32[]{:S(2)}, u32[]{:S(2)}) collective-permute-start(bf16[1,4,128,128]{3,2,1,0:T(8,128)(2,1)S(1)} %get-tuple-element.41), channel_id=1, source_target_pairs={{0,224},{32,0},{64,32},{96,64},{128,96},{160,128},{192,160},{224,1... | collective-permute-start | bytes 393224 | tf_op jit(solution)/shard_map/ppermute | solution.py:202
  60.9 0.0 collective-permute-start.10
  60.9 0.0 collective-permute-done.13.refs_2_
  60.9 3.7 %shard_map.46 = (f32[2,8,128,128]{3,2,1,0:T(8,128)S(1)}, f32[2,8,128,128]{3,2,1,0:T(8,128)S(1)}, f32[2,8,128,128]{3,2,1,0:T(8,128)S(1)}) custom-call(s32[4]{0:T(128)S(1)} %copy-done.2, bf16[2,8,128,128]{3,2,1,0:T(8,128)(2,1)S(1)} %get-tuple-element.31.rows_ref, ...), custom_call_target="tpu_custom_call", output_to_operand_aliasing={{0}: (5, {}), {1}: (6, {}), {2}: (7, {})} | custom-call | flops 2147483648 | bytes 4194304 | tf_op jit(solution)/shard_map/pallas_call | solution.py:134
  64.6 0.0 collective-permute-done.11.refs_1_
  64.6 1.6 %collective-permute-start.12 = (bf16[1,4,128,128]{3,2,1,0:T(8,128)(2,1)S(1)}, bf16[1,4,128,128]{3,2,1,0:T(8,128)(2,1)S(1)}, u32[]{:S(2)}, u32[]{:S(2)}) collective-permute-start(bf16[1,4,128,128]{3,2,1,0:T(8,128)(2,1)S(1)} %collective-permute-done.11.refs_1_), channel_id=1, source_target_pairs={{0,24},{8,0},{16,8},{24,16},{1,25},{9,1},{17,9},{25,17},{2,26},{10... | collective-permute-start | bytes 393224 | tf_op jit(solution)/shard_map/ppermute | solution.py:202
  66.2 0.0 collective-permute-done.14.refs_2_
  66.2 3.7 %shard_map.47 = (f32[2,8,128,128]{3,2,1,0:T(8,128)S(1)}, f32[2,8,128,128]{3,2,1,0:T(8,128)S(1)}, f32[2,8,128,128]{3,2,1,0:T(8,128)S(1)}) custom-call(s32[4]{0:T(128)S(1)} %copy-done.2, bf16[2,8,128,128]{3,2,1,0:T(8,128)(2,1)S(1)} %get-tuple-element.31.rows_ref, ...), custom_call_target="tpu_custom_call", output_to_operand_aliasing={{0}: (5, {}), {1}: (6, {}), {2}: (7, {})} | custom-call | flops 2147483648 | bytes 4194304 | tf_op jit(solution)/shard_map/pallas_call | solution.py:134
  69.9 0.0 collective-permute-done.12.refs_2_
  69.9 0.0 collective-permute-done.10.refs_0_
  69.9 3.0 %shard_map.48 = bf16[8,2,16,1024]{3,2,1,0:T(8,128)(2,1)S(1)} custom-call(s32[4]{0:T(128)S(1)} %copy-done.2, bf16[2,8,128,128]{3,2,1,0:T(8,128)(2,1)S(1)} %get-tuple-element.31.rows_ref, bf16[2,4,128,128]{3,2,1,0:T(8,128)(2,1)S(1)} %collective-permute-done.10.refs_0_, bf16[1,4,128,128]{3,2,1,0:T(8,128)(2,1)S(1)} %collective-permute-done.11.refs_1_, ...), custom_call_target="tpu_custom_call" | custom-call | flops 1073741824 | bytes 4194304 | tf_op jit(solution)/shard_map/pallas_call | solution.py:134
  73.0 17.7 %all_to_all.16.refs_0_ = bf16[8,2,16,1024]{3,2,1,0:T(8,128)(2,1)S(1)} all-to-all(bf16[8,2,16,1024]{3,2,1,0:T(8,128)(2,1)S(1)} %shard_map.48), channel_id=1, replica_groups=mesh['z'=8,'x'=4,'head'=8] {'head'}, dimensions={0} | all-to-all | bytes 1048576 | tf_op jit(solution)/shard_map/all_to_all | solution.py:206
  90.7 0.8 shard_map.49
  (5 shorter events, 0.0 us)
Async XLA Ops:
  0.0 0.9 copy-start.1
  12.0 11.7 %copy-start = (bf16[1,2,16,8192]{3,2,1,0:T(8,128)(2,1)S(1)}, bf16[1,2,16,8192]{3,2,1,0:T(8,128)(2,1)}, u32[]{:S(2)}) copy-start(bf16[1,2,16,8192]{3,2,1,0:T(8,128)(2,1)} %param.3) | copy-start | bytes 1572868
  12.0 5.4 %collective-permute-start = (bf16[1,4,128,128]{3,2,1,0:T(8,128)(2,1)S(1)}, bf16[1,4,128,128]{3,2,1,0:T(8,128)(2,1)S(1)}, u32[]{:S(2)}, u32[]{:S(2)}) collective-permute-start(bf16[1,4,128,128]{3,2,1,0:T(8,128)(2,1)S(1)} %shard_map.39.refs_0_), channel_id=1, source_target_pairs={{0,8},{8,16},{16,24},{24,0},{1,9},{9,17},{17,25},{25,1},{2,10},{10... | collective-permute-start | bytes 393224 | tf_op jit(solution)/shard_map/ppermute | solution.py:202
  13.3 4.1 %collective-permute-start.1 = (bf16[1,4,128,128]{3,2,1,0:T(8,128)(2,1)S(1)}, bf16[1,4,128,128]{3,2,1,0:T(8,128)(2,1)S(1)}, u32[]{:S(2)}, u32[]{:S(2)}) collective-permute-start(bf16[1,4,128,128]{3,2,1,0:T(8,128)(2,1)S(1)} %shard_map.39.refs_0_), channel_id=1, source_target_pairs={{0,24},{8,0},{16,8},{24,16},{1,25},{9,1},{17,9},{25,17},{2,26},{10... | collective-permute-start | bytes 393224 | tf_op jit(solution)/shard_map/ppermute | solution.py:202
  18.0 13.1 %collective-permute-start.3 = (bf16[3,4,128,128]{3,2,1,0:T(8,128)(2,1)S(1)}, bf16[3,4,128,128]{3,2,1,0:T(8,128)(2,1)S(1)}, u32[]{:S(2)}, u32[]{:S(2)}) collective-permute-start(bf16[3,4,128,128]{3,2,1,0:T(8,128)(2,1)S(1)} %shard_map.40.refs_0_), channel_id=1, source_target_pairs={{0,32},{32,64},{64,96},{96,128},{128,160},{160,192},{192,224},{224... | collective-permute-start | bytes 1179656 | tf_op jit(solution)/shard_map/ppermute | solution.py:202
  19.7 11.4 %collective-permute-start.5 = (bf16[3,4,128,128]{3,2,1,0:T(8,128)(2,1)S(1)}, bf16[3,4,128,128]{3,2,1,0:T(8,128)(2,1)S(1)}, u32[]{:S(2)}, u32[]{:S(2)}) collective-permute-start(bf16[3,4,128,128]{3,2,1,0:T(8,128)(2,1)S(1)} %shard_map.40.refs_0_), channel_id=1, source_target_pairs={{0,224},{32,0},{64,32},{96,64},{128,96},{160,128},{192,160},{224,1... | collective-permute-start | bytes 1179656 | tf_op jit(solution)/shard_map/ppermute | solution.py:202
  24.6 15.1 %all-to-all-start = ((bf16[8,16,16,128]{3,2,1,0:T(8,128)(2,1)}), bf16[8,16,16,128]{3,2,1,0:T(8,128)(2,1)S(1)}, u32[]{:S(2)}, u32[]{:S(2)}) async-start(bf16[8,16,16,128]{3,2,1,0:T(8,128)(2,1)} %shard_map.37), calls=%async_computation | async-start | bytes 1048576 | tf_op jit(solution)/shard_map/all_to_all | solution.py:206
  30.2 9.5 %copy-start.2 = (s32[4]{0:T(128)S(1)}, s32[4]{0:T(128)}, u32[]{:S(2)}) copy-start(s32[4]{0:T(128)} %docs_ref.9) | copy-start | bytes 52
  31.4 11.3 %collective-permute-start.7 = (bf16[2,4,128,128]{3,2,1,0:T(8,128)(2,1)S(1)}, bf16[2,4,128,128]{3,2,1,0:T(8,128)(2,1)S(1)}, u32[]{:S(2)}, u32[]{:S(2)}) collective-permute-start(bf16[2,4,128,128]{3,2,1,0:T(8,128)(2,1)S(1)} %shard_map.42), channel_id=1, source_target_pairs={{0,24},{8,0},{16,8},{24,16},{1,25},{9,1},{17,9},{25,17},{2,26},{10... | collective-permute-start | bytes 786440 | tf_op jit(solution)/shard_map/ppermute | solution.py:202
  33.5 5.3 %collective-permute-start.2 = (bf16[1,4,128,128]{3,2,1,0:T(8,128)(2,1)S(1)}, bf16[1,4,128,128]{3,2,1,0:T(8,128)(2,1)S(1)}, u32[]{:S(2)}, u32[]{:S(2)}) collective-permute-start(bf16[1,4,128,128]{3,2,1,0:T(8,128)(2,1)S(1)} %shard_map.39.refs_0_), channel_id=1, source_target_pairs={{0,16},{8,24},{16,0},{24,8},{1,17},{9,25},{17,1},{25,9},{2,18},{10... | collective-permute-start | bytes 393224 | tf_op jit(solution)/shard_map/ppermute | solution.py:202
  34.4 12.0 %collective-permute-start.4 = (bf16[3,4,128,128]{3,2,1,0:T(8,128)(2,1)S(1)}, bf16[3,4,128,128]{3,2,1,0:T(8,128)(2,1)S(1)}, u32[]{:S(2)}, u32[]{:S(2)}) collective-permute-start(bf16[3,4,128,128]{3,2,1,0:T(8,128)(2,1)S(1)} %collective-permute-done.3.refs_0_), channel_id=1, source_target_pairs={{0,32},{32,64},{64,96},{96,128},{128,160},{160,192},{192,224},{224... | collective-permute-start | bytes 1179656 | tf_op jit(solution)/shard_map/ppermute | solution.py:202
  34.4 12.0 %collective-permute-start.6 = (bf16[3,4,128,128]{3,2,1,0:T(8,128)(2,1)S(1)}, bf16[3,4,128,128]{3,2,1,0:T(8,128)(2,1)S(1)}, u32[]{:S(2)}, u32[]{:S(2)}) collective-permute-start(bf16[3,4,128,128]{3,2,1,0:T(8,128)(2,1)S(1)} %collective-permute-done.5.refs_1_), channel_id=1, source_target_pairs={{0,224},{32,0},{64,32},{96,64},{128,96},{160,128},{192,160},{224,1... | collective-permute-start | bytes 1179656 | tf_op jit(solution)/shard_map/ppermute | solution.py:202
  46.4 8.4 %collective-permute-start.8 = (bf16[3,4,128,128]{3,2,1,0:T(8,128)(2,1)S(1)}, bf16[3,4,128,128]{3,2,1,0:T(8,128)(2,1)S(1)}, u32[]{:S(2)}, u32[]{:S(2)}) collective-permute-start(bf16[3,4,128,128]{3,2,1,0:T(8,128)(2,1)S(1)} %collective-permute-done.4.refs_0_), channel_id=1, source_target_pairs={{0,32},{32,64},{64,96},{96,128},{128,160},{160,192},{192,224},{224... | collective-permute-start | bytes 1179656 | tf_op jit(solution)/shard_map/ppermute | solution.py:202
  46.5 8.3 %collective-permute-start.9 = (bf16[3,4,128,128]{3,2,1,0:T(8,128)(2,1)S(1)}, bf16[3,4,128,128]{3,2,1,0:T(8,128)(2,1)S(1)}, u32[]{:S(2)}, u32[]{:S(2)}) collective-permute-start(bf16[3,4,128,128]{3,2,1,0:T(8,128)(2,1)S(1)} %collective-permute-done.6.refs_1_), channel_id=1, source_target_pairs={{0,224},{32,0},{64,32},{96,64},{128,96},{160,128},{192,160},{224,1... | collective-permute-start | bytes 1179656 | tf_op jit(solution)/shard_map/ppermute | solution.py:202
  49.5 11.3 %collective-permute-start.13 = (bf16[2,4,128,128]{3,2,1,0:T(8,128)(2,1)S(1)}, bf16[2,4,128,128]{3,2,1,0:T(8,128)(2,1)S(1)}, u32[]{:S(2)}, u32[]{:S(2)}) collective-permute-start(bf16[2,4,128,128]{3,2,1,0:T(8,128)(2,1)S(1)} %shard_map.45), channel_id=1, source_target_pairs={{0,24},{8,0},{16,8},{24,16},{1,25},{9,1},{17,9},{25,17},{2,26},{10... | collective-permute-start | bytes 786440 | tf_op jit(solution)/shard_map/ppermute | solution.py:202
  55.4 10.8 %collective-permute-start.14 = (bf16[2,4,128,128]{3,2,1,0:T(8,128)(2,1)S(1)}, bf16[2,4,128,128]{3,2,1,0:T(8,128)(2,1)S(1)}, u32[]{:S(2)}, u32[]{:S(2)}) collective-permute-start(bf16[2,4,128,128]{3,2,1,0:T(8,128)(2,1)S(1)} %get-tuple-element.50), channel_id=1, source_target_pairs={{0,24},{8,0},{16,8},{24,16},{1,25},{9,1},{17,9},{25,17},{2,26},{10... | collective-permute-start | bytes 786440 | tf_op jit(solution)/shard_map/ppermute | solution.py:202
  58.5 6.1 %collective-permute-start.11 = (bf16[1,4,128,128]{3,2,1,0:T(8,128)(2,1)S(1)}, bf16[1,4,128,128]{3,2,1,0:T(8,128)(2,1)S(1)}, u32[]{:S(2)}, u32[]{:S(2)}) collective-permute-start(bf16[1,4,128,128]{3,2,1,0:T(8,128)(2,1)S(1)} %get-tuple-element.41), channel_id=1, source_target_pairs={{0,224},{32,0},{64,32},{96,64},{128,96},{160,128},{192,160},{224,1... | collective-permute-start | bytes 393224 | tf_op jit(solution)/shard_map/ppermute | solution.py:202
  60.9 9.1 %collective-permute-start.10 = (bf16[2,4,128,128]{3,2,1,0:T(8,128)(2,1)S(1)}, bf16[2,4,128,128]{3,2,1,0:T(8,128)(2,1)S(1)}, u32[]{:S(2)}, u32[]{:S(2)}) collective-permute-start(bf16[2,4,128,128]{3,2,1,0:T(8,128)(2,1)S(1)} %get-tuple-element.40), channel_id=1, source_target_pairs={{0,32},{32,64},{64,96},{96,128},{128,160},{160,192},{192,224},{224... | collective-permute-start | bytes 786440 | tf_op jit(solution)/shard_map/ppermute | solution.py:202
  64.6 5.3 %collective-permute-start.12 = (bf16[1,4,128,128]{3,2,1,0:T(8,128)(2,1)S(1)}, bf16[1,4,128,128]{3,2,1,0:T(8,128)(2,1)S(1)}, u32[]{:S(2)}, u32[]{:S(2)}) collective-permute-start(bf16[1,4,128,128]{3,2,1,0:T(8,128)(2,1)S(1)} %collective-permute-done.11.refs_1_), channel_id=1, source_target_pairs={{0,24},{8,0},{16,8},{24,16},{1,25},{9,1},{17,9},{25,17},{2,26},{10... | collective-permute-start | bytes 393224 | tf_op jit(solution)/shard_map/ppermute | solution.py:202
where the time goes:
time: 92 us; the launch traced here: 91.7 us
  starting transfers between devices  32.4 us (35%)
  blocking collectives  28.7 us (31%)
  Pallas kernels  20.6 us (22%)
  waiting for transfers between devices  8.77 us (10%)
    all_to_all x2, blocking collectives, exchange(): return lax.all_to_all(x, 'head', split_axis=0, concat_axis=0, tiled=True)  28.7 us
    ppermute x15, starting transfers between devices, shift(): return lax.ppermute(x, axis, [(i, (i + by) % size) for i in range(size)])  26.7 us
    pallas_call x5, Pallas kernels, run(): pl.pallas_call(functools.partial(attend, steps, refs, first, last), out_s...  17.1 us
    ppermute x15, waiting for transfers between devices, shift(): return lax.ppermute(x, axis, [(i, (i + by) % size) for i in range(size)])  7.89 us
    all_to_all x1, starting transfers between devices, exchange(): return lax.all_to_all(x, 'head', split_axis=0, concat_axis=0, tiled=True)  5.63 us
    pallas_call x5, Pallas kernels, moved(): pl.pallas_call(body, out_shape=[jax.ShapeDtypeStruct(shape, jnp.bfloat16)...  2.58 us
  transfers between devices with their start and end apart: 16, of which 5 were waited for; matrix products, arithmetic and copies ran while one was open for 0% of the time, Pallas kernels for 18%

commit v1 on v0

--- a/solution.py
+++ b/solution.py
@@ -24,7 +24,7 @@
 def attend(steps, count, first, last, docs_ref, rows_ref, *refs):
     sent, refs = refs[:count], refs[count:]
     if not first:
-        old, refs = refs[:3], refs[3:]
+        refs = refs[3:]
     if last:
         out_ref, refs = refs[0], refs[1:]
     max_ref, sum_ref, acc_ref = refs[:3]
@@ -38,9 +38,6 @@
         max_ref[...] = jnp.full_like(max_ref, FAR)
         sum_ref[...] = jnp.zeros_like(sum_ref)
         acc_ref[...] = jnp.zeros_like(acc_ref)
-    elif last:
-        for ref, kept in zip(refs[:3], old):
-            ref[...] = kept[...]
     tilt = lax.broadcasted_iota(jnp.int32, (BLK, BLK), 1) - lax.broadcasted_iota(
         jnp.int32, (BLK, BLK), 0
     )
@@ -67,11 +64,8 @@
                 keys = jnp.concatenate([ref[side] for ref in blocks], axis=0)
                 values = jnp.concatenate([ref[2 + side] for ref in blocks], axis=0)
                 rows = rows_ref[half].reshape(GROUP * BLK, HEAD_WIDTH)
-                scores = (
-                    lax.dot_general(
-                        rows, keys, (((1,), (1,)), ((), ())), preferred_element_type=jnp.float32
-                    )
-                    * SCALE
+                scores = lax.dot_general(
+                    rows, keys, (((1,), (1,)), ((), ())), preferred_element_type=jnp.float32
                 )
                 parts = [
                     scores[:, d * BLK : (d + 1) * BLK].reshape(GROUP, BLK, BLK) for d in range(X)
@@ -85,8 +79,8 @@
                 top = functools.reduce(jnp.maximum, parts)
                 before = max_ref[half]
                 now = jnp.maximum(before, jnp.max(top, axis=2, keepdims=True))
-                fade = jnp.exp2(before - now)
-                parts = [jnp.exp2(part - now) for part in parts]
+                fade = jnp.exp2((before - now) * SCALE)
+                parts = [jnp.exp2((part - now) * SCALE) for part in parts]
                 max_ref[half] = now
                 sum_ref[half] = sum_ref[half] * fade + functools.reduce(jnp.add, parts)
                 weights = jnp.concatenate([part.astype(jnp.bfloat16) for part in parts], axis=2)
@@ -121,22 +115,19 @@
     vmem = pl.BlockSpec(memory_space=pltpu.VMEM)
     kept = [] if first else list(state)
     refs = len(bundles)
+    out_shape = [jax.ShapeDtypeStruct(state_shape, jnp.float32)] * 3
+    at, offset = 2 + refs, 1 if last else 0
+    aliases = {} if first else {at + i: offset + i for i in range(3)}
+    if first:
+        out_shape = [*out_shape, jax.ShapeDtypeStruct(state_shape, jnp.bfloat16)]
     if last:
-        out_shape = jax.ShapeDtypeStruct(shape, jnp.bfloat16)
-        out_specs, scratch, aliases = vmem, [pltpu.VMEM(state_shape, jnp.float32)] * 3, {}
-    else:
-        out_shape = [jax.ShapeDtypeStruct(state_shape, jnp.float32)] * 3
-        if first:
-            out_shape.append(jax.ShapeDtypeStruct(state_shape, jnp.bfloat16))
-        out_specs, scratch = [vmem] * len(out_shape), []
-        aliases = {} if first else {2 + refs + i: i for i in range(3)}
+        out_shape = [jax.ShapeDtypeStruct(shape, jnp.bfloat16), *out_shape]
     pairs = 4 * len(steps)
     return pl.pallas_call(
         functools.partial(attend, steps, refs, first, last),
         out_shape=out_shape,
         in_specs=[pl.BlockSpec(memory_space=pltpu.SMEM)] + [vmem] * (1 + refs + len(kept)),
-        out_specs=out_specs,
-        scratch_shapes=scratch,
+        out_specs=[vmem] * len(out_shape),
         input_output_aliases=aliases,
         compiler_params=pltpu.CompilerParams(vmem_limit_bytes=20 * 2**20),
         cost_estimate=pl.CostEstimate(
@@ -224,29 +215,30 @@
     [trio] = moved([(i, 0, 0, i) for i in range(3)], [near, *beside], [(3, *block)])
 
     picks = [(0, 0), (0, 1), (0, 2), (1, 0)]
+    up, down = shift(trio, "z", Z, 1), shift(trio, "z", Z, -1)
+    (up, down), q, far = lax.optimization_barrier(((up, down), q, far))
     *state, q = run(doc_blocks, q, [(0, picks)], [trio, far], None, False)
-    up = down = trio
     for k in range(1, Z // 2):
-        up, down = shift(up, "z", Z, 1), shift(down, "z", Z, -1)
         both = [(0, 2, 0, 0), (1, 2, 0, 1)]
         if k < Z // 2 - 1:
             [cross] = moved(both, [up, down], [(2, *block)])
+            ahead, behind = up, down
         else:
-            cross, pair, lone = moved(
+            cross, ahead, behind = moved(
                 [*both, (0, pl.ds(0, 2), 1, every), (1, 2, 2, 0)],
                 [up, down],
                 [(2, *block), (2, *block), (1, *block)],
             )
+        following = shift(ahead, "z", Z, 1), shift(behind, "z", Z, -1)
         cross = shift(cross, "x", X, -1)
         picks = [[(side, 0), (side, 1), (side, 2), (2, side)] for side in range(2)]
         steps = [(-k, picks[0]), (k, picks[1])]
-        if k > 1:
-            (up, down), state = lax.optimization_barrier(((up, down), state))
+        following, state = lax.optimization_barrier((following, state))
         state = run(doc_blocks, q, steps, [up, down, cross], state, False)
-    pair, lone = shift(pair, "z", Z, 1), shift(lone, "z", Z, -1)
-    cross = shift(lone, "x", X, -1)
+        up, down = following
+    cross = shift(down, "x", X, -1)
     picks = [(0, 0), (0, 1), (1, 0), (2, 0)]
-    out = run(doc_blocks, q, [(-(Z // 2), picks)], [pair, lone, cross], state, True, shape)
+    out, *_ = run(doc_blocks, q, [(-(Z // 2), picks)], [up, down, cross], state, True, shape)
 
     out = exchange(out)
     [out] = moved(

time: 92 us -> 91.8 us (level)
  Pallas kernels: 20.6 us -> 9.74 us
  starting transfers between devices: 32.4 us -> 38.5 us
  waiting for transfers between devices: 8.77 us -> 11.4 us
  blocking collectives: 28.7 us -> 29.8 us
    pallas_call x5, Pallas kernels: 17.1 us -> 6.24 us  [run(): pl.pallas_call(functools.partial(attend, steps, refs, first, last), out_s...]
    ppermute x15, starting transfers between devices: 26.7 us -> 34 us  [shift(): return lax.ppermute(x, axis, [(i, (i + by) % size) for i in range(size)])]
    ppermute x15, waiting for transfers between devices: 7.89 us -> 11.4 us  [shift(): return lax.ppermute(x, axis, [(i, (i + by) % size) for i in range(size)])]
    all_to_all x2, blocking collectives: 28.7 us -> 29.8 us  [exchange(): return lax.all_to_all(x, 'head', split_axis=0, concat_axis=0, tiled=True)]
    all_to_all x1, starting transfers between devices: 5.63 us -> 4.54 us  [exchange(): return lax.all_to_all(x, 'head', split_axis=0, concat_axis=0, tiled=True)]
  transfers between devices with their start and end apart: 16 -> 16, of which waited for: 5 -> 6; matrix products, arithmetic and copies ran while one was open for 0% -> 0% of each run, Pallas kernels for 18% -> 9%
where the time goes in v1:
time: 91.8 us; the launch traced here: 90.8 us
  starting transfers between devices  38.5 us (42%)
  blocking collectives  29.8 us (32%)
  waiting for transfers between devices  11.4 us (12%)
  Pallas kernels  9.74 us (11%)
  local copies, waits for them, and re-layouts  0.97 us (1%)
    ppermute x15, starting transfers between devices, shift(): return lax.ppermute(x, axis, [(i, (i + by) % size) for i in range(size)])  34 us
    all_to_all x2, blocking collectives, exchange(): return lax.all_to_all(x, 'head', split_axis=0, concat_axis=0, tiled=True)  29.8 us
    ppermute x15, waiting for transfers between devices, shift(): return lax.ppermute(x, axis, [(i, (i + by) % size) for i in range(size)])  11.4 us
    pallas_call x5, Pallas kernels, run(): pl.pallas_call(functools.partial(attend, steps, refs, first, last), out_s...  6.24 us
    all_to_all x1, starting transfers between devices, exchange(): return lax.all_to_all(x, 'head', split_axis=0, concat_axis=0, tiled=True)  4.54 us
    pallas_call x5, Pallas kernels, moved(): pl.pallas_call(body, out_shape=[jax.ShapeDtypeStruct(shape, jnp.bfloat16)...  2.58 us
  transfers between devices with their start and end apart: 16, of which 6 were waited for; matrix products, arithmetic and copies ran while one was open for 0% of the time, Pallas kernels for 9%

profile of v1, /device:TPU:1, one launch (start us, length us, event | category | flops | bytes accessed | tf_op | source)
XLA Modules:
  0.0 90.8 jit_solution(13519457532683507810)
XLA Ops:
  0.0 1.0 %copy-done.1 = bf16[1,2,2,16,1024]{4,3,2,1,0:T(8,128)(2,1)S(1)} copy-done((bf16[1,2,2,16,1024]{4,3,2,1,0:T(8,128)(2,1)S(1)}, bf16[1,2,2,16,1024]{4,3,2,1,0:T(8,128)(2,1)}, u32[]{:S(2)}) %copy-start.1) | copy-done | bytes 131096
  1.0 11.0 %all_to_all.15.in_ref = bf16[8,4,16,128]{3,2,1,0:T(8,128)(2,1)S(1)} all-to-all(bf16[8,4,16,128]{3,2,1,0:T(8,128)(2,1)S(1)} %shard_map.37), channel_id=1, replica_groups=mesh['z'=8,'x'=4,'head'=8] {'head'}, dimensions={0} | all-to-all | bytes 262144 | tf_op jit(solution)/shard_map/all_to_all | solution.py:197
  12.0 2.6 %collective-permute-start.1 = (bf16[1,4,128,128]{3,2,1,0:T(8,128)(2,1)S(1)}, bf16[1,4,128,128]{3,2,1,0:T(8,128)(2,1)S(1)}, u32[]{:S(2)}, u32[]{:S(2)}) collective-permute-start(bf16[1,4,128,128]{3,2,1,0:T(8,128)(2,1)S(1)} %shard_map.38.refs_0_), channel_id=1, source_target_pairs={{0,24},{8,0},{16,8},{24,16},{1,25},{9,1},{17,9},{25,17},{2,26},{10... | collective-permute-start | bytes 393224 | tf_op jit(solution)/shard_map/ppermute | solution.py:193
  14.6 0.0 collective-permute-start
  14.6 0.0 copy-done
  14.6 0.9 shard_map.40
  15.5 4.5 %all-to-all-start.1 = ((bf16[8,16,16,128]{3,2,1,0:T(8,128)(2,1)}), bf16[8,16,16,128]{3,2,1,0:T(8,128)(2,1)S(1)}, u32[]{:S(2)}, u32[]{:S(2)}) async-start(bf16[8,16,16,128]{3,2,1,0:T(8,128)(2,1)} %shard_map.40), calls=%async_computation.1 | async-start | bytes 1048576 | tf_op jit(solution)/shard_map/all_to_all | solution.py:197
  20.0 0.0 collective-permute-done.1.refs_2_
  20.0 0.0 collective-permute-done.refs_1_
  20.0 0.5 shard_map.39.refs_0_
  20.6 0.0 copy-start.2
  20.6 5.7 %collective-permute-start.3 = (bf16[3,4,128,128]{3,2,1,0:T(8,128)(2,1)S(1)}, bf16[3,4,128,128]{3,2,1,0:T(8,128)(2,1)S(1)}, u32[]{:S(2)}, u32[]{:S(2)}) collective-permute-start(bf16[3,4,128,128]{3,2,1,0:T(8,128)(2,1)S(1)} %shard_map.39.refs_0_), channel_id=1, source_target_pairs={{0,224},{32,0},{64,32},{96,64},{128,96},{160,128},{192,160},{224,1... | collective-permute-start | bytes 1179656 | tf_op jit(solution)/shard_map/ppermute | solution.py:193
  26.3 0.0 collective-permute-start.2
  26.3 2.0 %collective-permute-start.4 = (bf16[1,4,128,128]{3,2,1,0:T(8,128)(2,1)S(1)}, bf16[1,4,128,128]{3,2,1,0:T(8,128)(2,1)S(1)}, u32[]{:S(2)}, u32[]{:S(2)}) collective-permute-start(bf16[1,4,128,128]{3,2,1,0:T(8,128)(2,1)S(1)} %shard_map.38.refs_0_), channel_id=1, source_target_pairs={{0,16},{8,24},{16,0},{24,8},{1,17},{9,25},{17,1},{25,9},{2,18},{10... | collective-permute-start | bytes 393224 | tf_op jit(solution)/shard_map/ppermute | solution.py:193
  28.3 3.3 %collective-permute-done.4.refs_1_ = bf16[1,4,128,128]{3,2,1,0:T(8,128)(2,1)S(1)} collective-permute-done((bf16[1,4,128,128]{3,2,1,0:T(8,128)(2,1)S(1)}, bf16[1,4,128,128]{3,2,1,0:T(8,128)(2,1)S(1)}, u32[]{:S(2)}, u32[]{:S(2)}) %collective-permute-start.4) | collective-permute-done | bytes 131104 | tf_op jit(solution)/shard_map/ppermute | solution.py:193
  31.6 0.0 all-to-all-done.1.rows_ref
  31.6 1.2 %collective-permute-done.3.refs_1_ = bf16[3,4,128,128]{3,2,1,0:T(8,128)(2,1)S(1)} collective-permute-done((bf16[3,4,128,128]{3,2,1,0:T(8,128)(2,1)S(1)}, bf16[3,4,128,128]{3,2,1,0:T(8,128)(2,1)S(1)}, u32[]{:S(2)}, u32[]{:S(2)}) %collective-permute-start.3) | collective-permute-done | bytes 393248 | tf_op jit(solution)/shard_map/ppermute | solution.py:193
  32.8 3.1 %collective-permute-done.2.refs_0_ = bf16[3,4,128,128]{3,2,1,0:T(8,128)(2,1)S(1)} collective-permute-done((bf16[3,4,128,128]{3,2,1,0:T(8,128)(2,1)S(1)}, bf16[3,4,128,128]{3,2,1,0:T(8,128)(2,1)S(1)}, u32[]{:S(2)}, u32[]{:S(2)}) %collective-permute-start.2) | collective-permute-done | bytes 393248 | tf_op jit(solution)/shard_map/ppermute | solution.py:193
  35.9 0.0 collective-permute-start.5
  35.9 2.7 %collective-permute-start.6 = (bf16[3,4,128,128]{3,2,1,0:T(8,128)(2,1)S(1)}, bf16[3,4,128,128]{3,2,1,0:T(8,128)(2,1)S(1)}, u32[]{:S(2)}, u32[]{:S(2)}) collective-permute-start(bf16[3,4,128,128]{3,2,1,0:T(8,128)(2,1)S(1)} %collective-permute-done.3.refs_1_), channel_id=1, source_target_pairs={{0,224},{32,0},{64,32},{96,64},{128,96},{160,128},{192,160},{224,1... | collective-permute-start | bytes 1179656 | tf_op jit(solution)/shard_map/ppermute | solution.py:193
  38.6 0.3 shard_map.42
  39.0 4.8 %collective-permute-start.9 = (bf16[2,4,128,128]{3,2,1,0:T(8,128)(2,1)S(1)}, bf16[2,4,128,128]{3,2,1,0:T(8,128)(2,1)S(1)}, u32[]{:S(2)}, u32[]{:S(2)}) collective-permute-start(bf16[2,4,128,128]{3,2,1,0:T(8,128)(2,1)S(1)} %shard_map.42), channel_id=1, source_target_pairs={{0,24},{8,0},{16,8},{24,16},{1,25},{9,1},{17,9},{25,17},{2,26},{10... | collective-permute-start | bytes 786440 | tf_op jit(solution)/shard_map/ppermute | solution.py:193
  43.8 3.0 %shard_map.41 = (f32[2,8,128,128]{3,2,1,0:T(8,128)S(1)}, f32[2,8,128,128]{3,2,1,0:T(8,128)S(1)}, f32[2,8,128,128]{3,2,1,0:T(8,128)S(1)}, bf16[2,8,128,128]{3,2,1,0:T(8,128)(2,1)S(1)}) custom-call(s32[4]{0:T(128)S(1)} %copy-done.2, bf16[8,16,16,128]{3,2,1,0:T(8,128)(2,1)S(1)} %all-to-all-done.1.rows_ref, bf16[3,4,128,128]{3,2,1,0:T(8,128)(2,1)S(1)} %shard_map.39.refs_0_, ...), custom_call_target="tpu_custom_call" | custom-call | flops 1073741824 | bytes 4194304 | tf_op jit(solution)/shard_map/pallas_call | solution.py:126
  46.7 0.0 collective-permute-done.5.refs_0_
  46.7 0.0 collective-permute-done.6.refs_1_
  46.8 0.1 collective-permute-start.7
  46.8 2.7 %collective-permute-start.8 = (bf16[3,4,128,128]{3,2,1,0:T(8,128)(2,1)S(1)}, bf16[3,4,128,128]{3,2,1,0:T(8,128)(2,1)S(1)}, u32[]{:S(2)}, u32[]{:S(2)}) collective-permute-start(bf16[3,4,128,128]{3,2,1,0:T(8,128)(2,1)S(1)} %collective-permute-done.6.refs_1_), channel_id=1, source_target_pairs={{0,224},{32,0},{64,32},{96,64},{128,96},{160,128},{192,160},{224,1... | collective-permute-start | bytes 1179656 | tf_op jit(solution)/shard_map/ppermute | solution.py:193
  49.5 0.3 shard_map.45
  49.8 4.7 %collective-permute-start.12 = (bf16[2,4,128,128]{3,2,1,0:T(8,128)(2,1)S(1)}, bf16[2,4,128,128]{3,2,1,0:T(8,128)(2,1)S(1)}, u32[]{:S(2)}, u32[]{:S(2)}) collective-permute-start(bf16[2,4,128,128]{3,2,1,0:T(8,128)(2,1)S(1)} %shard_map.45), channel_id=1, source_target_pairs={{0,24},{8,0},{16,8},{24,16},{1,25},{9,1},{17,9},{25,17},{2,26},{10... | collective-permute-start | bytes 786440 | tf_op jit(solution)/shard_map/ppermute | solution.py:193
  54.5 0.0 collective-permute-done.9.refs_2_
  54.5 0.8 shard_map.43
  55.3 1.3 %collective-permute-done.7.refs_0_ = bf16[3,4,128,128]{3,2,1,0:T(8,128)(2,1)S(1)} collective-permute-done((bf16[3,4,128,128]{3,2,1,0:T(8,128)(2,1)S(1)}, bf16[3,4,128,128]{3,2,1,0:T(8,128)(2,1)S(1)}, u32[]{:S(2)}, u32[]{:S(2)}) %collective-permute-start.7) | collective-permute-done | bytes 393248 | tf_op jit(solution)/shard_map/ppermute | solution.py:193
  56.5 0.0 collective-permute-done.8.refs_1_
  56.5 0.5 shard_map.44
  57.1 0.1 collective-permute-start.10
  57.2 4.4 %collective-permute-start.14 = (bf16[2,4,128,128]{3,2,1,0:T(8,128)(2,1)S(1)}, bf16[2,4,128,128]{3,2,1,0:T(8,128)(2,1)S(1)}, u32[]{:S(2)}, u32[]{:S(2)}) collective-permute-start(bf16[2,4,128,128]{3,2,1,0:T(8,128)(2,1)S(1)} %get-tuple-element.69), channel_id=1, source_target_pairs={{0,24},{8,0},{16,8},{24,16},{1,25},{9,1},{17,9},{25,17},{2,26},{10... | collective-permute-start | bytes 786440 | tf_op jit(solution)/shard_map/ppermute | solution.py:193
  61.6 2.6 %collective-permute-start.11 = (bf16[1,4,128,128]{3,2,1,0:T(8,128)(2,1)S(1)}, bf16[1,4,128,128]{3,2,1,0:T(8,128)(2,1)S(1)}, u32[]{:S(2)}, u32[]{:S(2)}) collective-permute-start(bf16[1,4,128,128]{3,2,1,0:T(8,128)(2,1)S(1)} %get-tuple-element.60), channel_id=1, source_target_pairs={{0,224},{32,0},{64,32},{96,64},{128,96},{160,128},{192,160},{224,1... | collective-permute-start | bytes 393224 | tf_op jit(solution)/shard_map/ppermute | solution.py:193
  64.2 0.0 collective-permute-done.12.refs_2_
  64.2 0.8 shard_map.46
  65.0 1.2 %collective-permute-done.11.refs_1_ = bf16[1,4,128,128]{3,2,1,0:T(8,128)(2,1)S(1)} collective-permute-done((bf16[1,4,128,128]{3,2,1,0:T(8,128)(2,1)S(1)}, bf16[1,4,128,128]{3,2,1,0:T(8,128)(2,1)S(1)}, u32[]{:S(2)}, u32[]{:S(2)}) %collective-permute-start.11) | collective-permute-done | bytes 131104 | tf_op jit(solution)/shard_map/ppermute | solution.py:193
  66.1 0.0 collective-permute-done.10.refs_0_
  66.1 1.8 %collective-permute-start.13 = (bf16[1,4,128,128]{3,2,1,0:T(8,128)(2,1)S(1)}, bf16[1,4,128,128]{3,2,1,0:T(8,128)(2,1)S(1)}, u32[]{:S(2)}, u32[]{:S(2)}) collective-permute-start(bf16[1,4,128,128]{3,2,1,0:T(8,128)(2,1)S(1)} %collective-permute-done.11.refs_1_), channel_id=1, source_target_pairs={{0,24},{8,0},{16,8},{24,16},{1,25},{9,1},{17,9},{25,17},{2,26},{10... | collective-permute-start | bytes 393224 | tf_op jit(solution)/shard_map/ppermute | solution.py:193
  67.9 0.0 collective-permute-done.14.refs_2_
  67.9 0.8 shard_map.47
  68.7 1.3 %collective-permute-done.13.refs_2_ = bf16[1,4,128,128]{3,2,1,0:T(8,128)(2,1)S(1)} collective-permute-done((bf16[1,4,128,128]{3,2,1,0:T(8,128)(2,1)S(1)}, bf16[1,4,128,128]{3,2,1,0:T(8,128)(2,1)S(1)}, u32[]{:S(2)}, u32[]{:S(2)}) %collective-permute-start.13) | collective-permute-done | bytes 131104 | tf_op jit(solution)/shard_map/ppermute | solution.py:193
  70.0 1.0 %shard_map.48 = (bf16[8,2,16,1024]{3,2,1,0:T(8,128)(2,1)S(1)}, f32[2,8,128,128]{3,2,1,0:T(8,128)S(1)}, f32[2,8,128,128]{3,2,1,0:T(8,128)S(1)}, f32[2,8,128,128]{3,2,1,0:T(8,128)S(1)}) custom-call(s32[4]{0:T(128)S(1)} %copy-done.2, ...), custom_call_target="tpu_custom_call", output_to_operand_aliasing={{1}: (5, {}), {2}: (6, {}), {3}: (7, {})} | custom-call | flops 1073741824 | bytes 4194304 | tf_op jit(solution)/shard_map/pallas_call | solution.py:126
  71.0 18.8 %all_to_all.16.refs_0_ = bf16[8,2,16,1024]{3,2,1,0:T(8,128)(2,1)S(1)} all-to-all(bf16[8,2,16,1024]{3,2,1,0:T(8,128)(2,1)S(1)} %get-tuple-element.76), channel_id=1, replica_groups=mesh['z'=8,'x'=4,'head'=8] {'head'}, dimensions={0} | all-to-all | bytes 1048576 | tf_op jit(solution)/shard_map/all_to_all | solution.py:197
  89.8 0.8 shard_map.49
  (5 shorter events, 0.0 us)
Async XLA Ops:
  0.0 14.6 %copy-start = (bf16[1,2,16,8192]{3,2,1,0:T(8,128)(2,1)S(1)}, bf16[1,2,16,8192]{3,2,1,0:T(8,128)(2,1)}, u32[]{:S(2)}) copy-start(bf16[1,2,16,8192]{3,2,1,0:T(8,128)(2,1)} %param.3) | copy-start | bytes 1572868
  0.0 1.0 %copy-start.1 = (bf16[1,2,2,16,1024]{4,3,2,1,0:T(8,128)(2,1)S(1)}, bf16[1,2,2,16,1024]{4,3,2,1,0:T(8,128)(2,1)}, u32[]{:S(2)}) copy-start(bf16[1,2,2,16,1024]{4,3,2,1,0:T(8,128)(2,1)} %param.4) | copy-start | bytes 393220
  12.0 8.0 %collective-permute-start.1 = (bf16[1,4,128,128]{3,2,1,0:T(8,128)(2,1)S(1)}, bf16[1,4,128,128]{3,2,1,0:T(8,128)(2,1)S(1)}, u32[]{:S(2)}, u32[]{:S(2)}) collective-permute-start(bf16[1,4,128,128]{3,2,1,0:T(8,128)(2,1)S(1)} %shard_map.38.refs_0_), channel_id=1, source_target_pairs={{0,24},{8,0},{16,8},{24,16},{1,25},{9,1},{17,9},{25,17},{2,26},{10... | collective-permute-start | bytes 393224 | tf_op jit(solution)/shard_map/ppermute | solution.py:193
  14.6 5.4 %collective-permute-start = (bf16[1,4,128,128]{3,2,1,0:T(8,128)(2,1)S(1)}, bf16[1,4,128,128]{3,2,1,0:T(8,128)(2,1)S(1)}, u32[]{:S(2)}, u32[]{:S(2)}) collective-permute-start(bf16[1,4,128,128]{3,2,1,0:T(8,128)(2,1)S(1)} %shard_map.38.refs_0_), channel_id=1, source_target_pairs={{0,8},{8,16},{16,24},{24,0},{1,9},{9,17},{17,25},{25,1},{2,10},{10... | collective-permute-start | bytes 393224 | tf_op jit(solution)/shard_map/ppermute | solution.py:193
  15.5 16.1 %all-to-all-start.1 = ((bf16[8,16,16,128]{3,2,1,0:T(8,128)(2,1)}), bf16[8,16,16,128]{3,2,1,0:T(8,128)(2,1)S(1)}, u32[]{:S(2)}, u32[]{:S(2)}) async-start(bf16[8,16,16,128]{3,2,1,0:T(8,128)(2,1)} %shard_map.40), calls=%async_computation.1 | async-start | bytes 1048576 | tf_op jit(solution)/shard_map/all_to_all | solution.py:197
  20.6 23.2 %copy-start.2 = (s32[4]{0:T(128)S(1)}, s32[4]{0:T(128)}, u32[]{:S(2)}) copy-start(s32[4]{0:T(128)} %docs_ref.9) | copy-start | bytes 52
  20.6 12.2 %collective-permute-start.3 = (bf16[3,4,128,128]{3,2,1,0:T(8,128)(2,1)S(1)}, bf16[3,4,128,128]{3,2,1,0:T(8,128)(2,1)S(1)}, u32[]{:S(2)}, u32[]{:S(2)}) collective-permute-start(bf16[3,4,128,128]{3,2,1,0:T(8,128)(2,1)S(1)} %shard_map.39.refs_0_), channel_id=1, source_target_pairs={{0,224},{32,0},{64,32},{96,64},{128,96},{160,128},{192,160},{224,1... | collective-permute-start | bytes 1179656 | tf_op jit(solution)/shard_map/ppermute | solution.py:193
  26.3 9.7 %collective-permute-start.2 = (bf16[3,4,128,128]{3,2,1,0:T(8,128)(2,1)S(1)}, bf16[3,4,128,128]{3,2,1,0:T(8,128)(2,1)S(1)}, u32[]{:S(2)}, u32[]{:S(2)}) collective-permute-start(bf16[3,4,128,128]{3,2,1,0:T(8,128)(2,1)S(1)} %shard_map.39.refs_0_), channel_id=1, source_target_pairs={{0,32},{32,64},{64,96},{96,128},{128,160},{160,192},{192,224},{224... | collective-permute-start | bytes 1179656 | tf_op jit(solution)/shard_map/ppermute | solution.py:193
  26.3 5.3 %collective-permute-start.4 = (bf16[1,4,128,128]{3,2,1,0:T(8,128)(2,1)S(1)}, bf16[1,4,128,128]{3,2,1,0:T(8,128)(2,1)S(1)}, u32[]{:S(2)}, u32[]{:S(2)}) collective-permute-start(bf16[1,4,128,128]{3,2,1,0:T(8,128)(2,1)S(1)} %shard_map.38.refs_0_), channel_id=1, source_target_pairs={{0,16},{8,24},{16,0},{24,8},{1,17},{9,25},{17,1},{25,9},{2,18},{10... | collective-permute-start | bytes 393224 | tf_op jit(solution)/shard_map/ppermute | solution.py:193
  35.9 10.8 %collective-permute-start.5 = (bf16[3,4,128,128]{3,2,1,0:T(8,128)(2,1)S(1)}, bf16[3,4,128,128]{3,2,1,0:T(8,128)(2,1)S(1)}, u32[]{:S(2)}, u32[]{:S(2)}) collective-permute-start(bf16[3,4,128,128]{3,2,1,0:T(8,128)(2,1)S(1)} %collective-permute-done.2.refs_0_), channel_id=1, source_target_pairs={{0,32},{32,64},{64,96},{96,128},{128,160},{160,192},{192,224},{224... | collective-permute-start | bytes 1179656 | tf_op jit(solution)/shard_map/ppermute | solution.py:193
  35.9 10.8 %collective-permute-start.6 = (bf16[3,4,128,128]{3,2,1,0:T(8,128)(2,1)S(1)}, bf16[3,4,128,128]{3,2,1,0:T(8,128)(2,1)S(1)}, u32[]{:S(2)}, u32[]{:S(2)}) collective-permute-start(bf16[3,4,128,128]{3,2,1,0:T(8,128)(2,1)S(1)} %collective-permute-done.3.refs_1_), channel_id=1, source_target_pairs={{0,224},{32,0},{64,32},{96,64},{128,96},{160,128},{192,160},{224,1... | collective-permute-start | bytes 1179656 | tf_op jit(solution)/shard_map/ppermute | solution.py:193
  39.0 15.6 %collective-permute-start.9 = (bf16[2,4,128,128]{3,2,1,0:T(8,128)(2,1)S(1)}, bf16[2,4,128,128]{3,2,1,0:T(8,128)(2,1)S(1)}, u32[]{:S(2)}, u32[]{:S(2)}) collective-permute-start(bf16[2,4,128,128]{3,2,1,0:T(8,128)(2,1)S(1)} %shard_map.42), channel_id=1, source_target_pairs={{0,24},{8,0},{16,8},{24,16},{1,25},{9,1},{17,9},{25,17},{2,26},{10... | collective-permute-start | bytes 786440 | tf_op jit(solution)/shard_map/ppermute | solution.py:193
  46.8 9.8 %collective-permute-start.7 = (bf16[3,4,128,128]{3,2,1,0:T(8,128)(2,1)S(1)}, bf16[3,4,128,128]{3,2,1,0:T(8,128)(2,1)S(1)}, u32[]{:S(2)}, u32[]{:S(2)}) collective-permute-start(bf16[3,4,128,128]{3,2,1,0:T(8,128)(2,1)S(1)} %collective-permute-done.5.refs_0_), channel_id=1, source_target_pairs={{0,32},{32,64},{64,96},{96,128},{128,160},{160,192},{192,224},{224... | collective-permute-start | bytes 1179656 | tf_op jit(solution)/shard_map/ppermute | solution.py:193
  46.8 9.7 %collective-permute-start.8 = (bf16[3,4,128,128]{3,2,1,0:T(8,128)(2,1)S(1)}, bf16[3,4,128,128]{3,2,1,0:T(8,128)(2,1)S(1)}, u32[]{:S(2)}, u32[]{:S(2)}) collective-permute-start(bf16[3,4,128,128]{3,2,1,0:T(8,128)(2,1)S(1)} %collective-permute-done.6.refs_1_), channel_id=1, source_target_pairs={{0,224},{32,0},{64,32},{96,64},{128,96},{160,128},{192,160},{224,1... | collective-permute-start | bytes 1179656 | tf_op jit(solution)/shard_map/ppermute | solution.py:193
  49.8 14.3 %collective-permute-start.12 = (bf16[2,4,128,128]{3,2,1,0:T(8,128)(2,1)S(1)}, bf16[2,4,128,128]{3,2,1,0:T(8,128)(2,1)S(1)}, u32[]{:S(2)}, u32[]{:S(2)}) collective-permute-start(bf16[2,4,128,128]{3,2,1,0:T(8,128)(2,1)S(1)} %shard_map.45), channel_id=1, source_target_pairs={{0,24},{8,0},{16,8},{24,16},{1,25},{9,1},{17,9},{25,17},{2,26},{10... | collective-permute-start | bytes 786440 | tf_op jit(solution)/shard_map/ppermute | solution.py:193
  57.1 9.0 %collective-permute-start.10 = (bf16[2,4,128,128]{3,2,1,0:T(8,128)(2,1)S(1)}, bf16[2,4,128,128]{3,2,1,0:T(8,128)(2,1)S(1)}, u32[]{:S(2)}, u32[]{:S(2)}) collective-permute-start(bf16[2,4,128,128]{3,2,1,0:T(8,128)(2,1)S(1)} %get-tuple-element.59), channel_id=1, source_target_pairs={{0,32},{32,64},{64,96},{96,128},{128,160},{160,192},{192,224},{224... | collective-permute-start | bytes 786440 | tf_op jit(solution)/shard_map/ppermute | solution.py:193
  57.2 10.8 %collective-permute-start.14 = (bf16[2,4,128,128]{3,2,1,0:T(8,128)(2,1)S(1)}, bf16[2,4,128,128]{3,2,1,0:T(8,128)(2,1)S(1)}, u32[]{:S(2)}, u32[]{:S(2)}) collective-permute-start(bf16[2,4,128,128]{3,2,1,0:T(8,128)(2,1)S(1)} %get-tuple-element.69), channel_id=1, source_target_pairs={{0,24},{8,0},{16,8},{24,16},{1,25},{9,1},{17,9},{25,17},{2,26},{10... | collective-permute-start | bytes 786440 | tf_op jit(solution)/shard_map/ppermute | solution.py:193
  61.6 4.5 %collective-permute-start.11 = (bf16[1,4,128,128]{3,2,1,0:T(8,128)(2,1)S(1)}, bf16[1,4,128,128]{3,2,1,0:T(8,128)(2,1)S(1)}, u32[]{:S(2)}, u32[]{:S(2)}) collective-permute-start(bf16[1,4,128,128]{3,2,1,0:T(8,128)(2,1)S(1)} %get-tuple-element.60), channel_id=1, source_target_pairs={{0,224},{32,0},{64,32},{96,64},{128,96},{160,128},{192,160},{224,1... | collective-permute-start | bytes 393224 | tf_op jit(solution)/shard_map/ppermute | solution.py:193
  66.1 3.9 %collective-permute-start.13 = (bf16[1,4,128,128]{3,2,1,0:T(8,128)(2,1)S(1)}, bf16[1,4,128,128]{3,2,1,0:T(8,128)(2,1)S(1)}, u32[]{:S(2)}, u32[]{:S(2)}) collective-permute-start(bf16[1,4,128,128]{3,2,1,0:T(8,128)(2,1)S(1)} %collective-permute-done.11.refs_1_), channel_id=1, source_target_pairs={{0,24},{8,0},{16,8},{24,16},{1,25},{9,1},{17,9},{25,17},{2,26},{10... | collective-permute-start | bytes 393224 | tf_op jit(solution)/shard_map/ppermute | solution.py:193

commit v2 on v1

--- a/solution.py
+++ b/solution.py
@@ -17,6 +17,7 @@
 SPAN_COUNT = 2 * Z * X
 CTX = ("z", "x")
 FAR = -1e30
+WIDE = 2
 ORDER = (0, 1, 3, 2)
 SCALE = HEAD_WIDTH ** (-0.5) * 1.4426950408889634
 
@@ -50,52 +51,73 @@
         end = end + docs_ref[j]
         starts = [jnp.where(end <= own, end, start) for own, start in zip(owns, starts)]
 
-    for away, picks in steps:
-        blocks = [sent[array].at[i] for array, i in picks]
-        z_index = lax.rem(my_z + away + Z, Z)
-
-        def pair(step, _, blocks=blocks, z_index=z_index):
-            half, side = step // 2, step % 2
-            start = jnp.where(half == 0, starts[0], starts[1])
-            own = jnp.where(half == 0, owns[0], owns[1])
-            low = jnp.where(side == 0, z_index * X, SPAN_COUNT - X - z_index * X)
-
-            def fold(masked):
-                keys = jnp.concatenate([ref[side] for ref in blocks], axis=0)
-                values = jnp.concatenate([ref[2 + side] for ref in blocks], axis=0)
-                rows = rows_ref[half].reshape(GROUP * BLK, HEAD_WIDTH)
-                scores = lax.dot_general(
-                    rows, keys, (((1,), (1,)), ((), ())), preferred_element_type=jnp.float32
+    chips = [
+        (lax.rem(my_z + away + Z, Z), [sent[array].at[i] for array, i in picks])
+        for away, picks in steps
+    ]
+
+    def pair(step, _):
+        half, side = step // 2, step % 2
+        start = jnp.where(half == 0, starts[0], starts[1])
+        own = jnp.where(half == 0, owns[0], owns[1])
+
+        def fold(blocks, chunk, low=None):
+            keys = jnp.concatenate([ref[side] for ref in blocks], axis=0)
+            values = jnp.concatenate([ref[2 + side] for ref in blocks], axis=0)
+            chunks = [pl.ds(g, chunk) for g in range(0, GROUP, chunk)]
+            scores = [
+                lax.dot_general(
+                    rows_ref[half, at].reshape(chunk * BLK, HEAD_WIDTH),
+                    keys,
+                    (((1,), (1,)), ((), ())),
+                    preferred_element_type=jnp.float32,
                 )
+                for at in chunks
+            ]
+            folded = []
+            for at, score in zip(chunks, scores):
                 parts = [
-                    scores[:, d * BLK : (d + 1) * BLK].reshape(GROUP, BLK, BLK) for d in range(X)
+                    score[:, d * BLK : (d + 1) * BLK].reshape(chunk, BLK, BLK)
+                    for d in range(len(blocks))
                 ]
-                if masked:
+                if low is not None:
                     for d in range(X):
                         place = lax.rem(x_index - ORDER[d] + X, X)
                         span = low + jnp.where(side == 0, place, X - 1 - place)
                         reach = jnp.where(span >= start, (own - span) * BLK, -2 * BLK)
                         parts[d] = jnp.where((tilt <= reach)[None], parts[d], 2 * FAR)
                 top = functools.reduce(jnp.maximum, parts)
-                before = max_ref[half]
+                before = max_ref[half, at]
                 now = jnp.maximum(before, jnp.max(top, axis=2, keepdims=True))
                 fade = jnp.exp2((before - now) * SCALE)
                 parts = [jnp.exp2((part - now) * SCALE) for part in parts]
-                max_ref[half] = now
-                sum_ref[half] = sum_ref[half] * fade + functools.reduce(jnp.add, parts)
+                max_ref[half, at] = now
+                sum_ref[half, at] = sum_ref[half, at] * fade + functools.reduce(jnp.add, parts)
                 weights = jnp.concatenate([part.astype(jnp.bfloat16) for part in parts], axis=2)
-                added = jnp.dot(
-                    weights.reshape(GROUP * BLK, X * BLK), values, preferred_element_type=jnp.float32
+                folded.append((fade, weights.reshape(chunk * BLK, len(blocks) * BLK)))
+            for at, (fade, weights) in zip(chunks, folded):
+                added = jnp.dot(weights, values, preferred_element_type=jnp.float32)
+                acc_ref[half, at] = acc_ref[half, at] * fade + added.reshape(
+                    chunk, BLK, HEAD_WIDTH
                 )
-                acc_ref[half] = acc_ref[half] * fade + added.reshape(GROUP, BLK, HEAD_WIDTH)
-
+
+        lows = [
+            jnp.where(side == 0, z_index * X, SPAN_COUNT - X - z_index * X) for z_index, _ in chips
+        ]
+        wholes = [(low + X <= own) & (low >= start) for low in lows]
+        every = functools.reduce(jnp.logical_and, wholes)
+        if len(chips) > 1:
+            pl.when(every)(lambda: fold([ref for _, blocks in chips for ref in blocks], WIDE))
+        for (_, blocks), low, whole in zip(chips, lows, wholes):
             touched = (low <= own) & (low + X > start)
-            whole = (low + X <= own) & (low >= start)
-            pl.when(whole)(lambda: fold(False))
-            pl.when(touched & jnp.logical_not(whole))(lambda: fold(True))
-            return 0
-
-        lax.fori_loop(0, 4, pair, 0)
+            alone = whole & jnp.logical_not(every) if len(chips) > 1 else whole
+            pl.when(alone)(lambda blocks=blocks: fold(blocks, GROUP))
+            pl.when(touched & jnp.logical_not(whole))(
+                lambda blocks=blocks, low=low: fold(blocks, GROUP, low)
+            )
+        return 0
+
+    lax.fori_loop(0, 4, pair, 0)
 
     if last:
         tokens = out_ref.shape[2]
@@ -136,14 +158,17 @@
     )(doc_blocks, query, *bundles, *kept)
 
 
-def moved(moves, operands, shapes):
+def moved(moves, operands, shapes, amount=None):
     left = pl.BlockSpec(memory_space=pl.ANY)
+    amount = amount or len(moves)
 
     def body(*refs):
         ins, outs, sem = refs[: len(operands)], refs[len(operands) : -1], refs[-1]
+        head = lax.axis_index("head")
+        listed = moves(lax.div(head, 2), lax.rem(head, 2)) if callable(moves) else moves
         copies = [
             pltpu.make_async_copy(ins[i].at[src], outs[o].at[dst], sem.at[n])
-            for n, (i, src, o, dst) in enumerate(moves)
+            for n, (i, src, o, dst) in enumerate(listed)
         ]
         for copy in copies:
             copy.start()
@@ -155,7 +180,7 @@
         out_shape=[jax.ShapeDtypeStruct(shape, jnp.bfloat16) for shape in shapes],
         in_specs=[left] * len(operands),
         out_specs=[left] * len(shapes),
-        scratch_shapes=[pltpu.SemaphoreType.DMA((len(moves),))],
+        scratch_shapes=[pltpu.SemaphoreType.DMA((amount,))],
         compiler_params=pltpu.CompilerParams(vmem_limit_bytes=2**20),
         cost_estimate=pl.CostEstimate(flops=0, bytes_accessed=2**20, transcendentals=0),
     )(*operands)
@@ -191,6 +216,53 @@
 
 def shift(x, axis, size, by):
     return lax.ppermute(x, axis, [(i, (i + by) % size) for i in range(size)])
+
+
+def returned(out):
+    heads, _, tokens, wide = out.shape
+    chips = heads // 2
+    every = slice(None)
+
+    def onward(y, to):
+        return lax.rem(y + to + chips, chips)
+
+    def across(y, core):
+        return [(0, 2 * to + 1 - core, 0, to) for to in range(chips)]
+
+    [other] = moved(across, [out], [(chips, *out.shape[1:])], chips)
+    other = lax.ppermute(other, "head", [(h, h ^ 1) for h in range(heads)])
+
+    def along(y, core):
+        listed = []
+        for to in range(1, chips):
+            at = onward(y, to)
+            listed += [(0, 2 * at + core, to - 1, core), (1, at, to - 1, 1 - core)]
+        return listed
+
+    pairs = moved(along, [out, other], [(2, *out.shape[1:])] * (chips - 1), 2 * (chips - 1))
+    came = {
+        to: lax.ppermute(
+            pairs[to - 1], "head", [(h, (h + 2 * to) % heads) for h in range(heads)]
+        )
+        for to in (2, 1, 3)
+    }
+
+    def placed(y, core):
+        def columns(head):
+            return (every, every, pl.ds(pl.multiple_of(head * wide, wide), wide))
+
+        listed = [
+            (0, 2 * y + core, 0, columns(2 * y + core)),
+            (1, y, 0, columns(2 * y + 1 - core)),
+        ]
+        for to in range(1, chips):
+            home = onward(y, -to)
+            listed += [(1 + to, e, 0, columns(2 * home + e)) for e in range(2)]
+        return listed
+
+    arrays = [out, other, *(came[to] for to in range(1, chips))]
+    [out] = moved(placed, arrays, [(2, tokens, heads * wide)], heads)
+    return out
 
 
 def exchange(x):
@@ -240,12 +312,7 @@
     picks = [(0, 0), (0, 1), (1, 0), (2, 0)]
     out, *_ = run(doc_blocks, q, [(-(Z // 2), picks)], [up, down, cross], state, True, shape)
 
-    out = exchange(out)
-    [out] = moved(
-        [(0, h, 0, (every, every, pl.ds(h * wide, wide))) for h in range(KEY_VALUE_HEADS)],
-        [out],
-        [(2, tokens, KEY_VALUE_HEADS * wide)],
-    )
+    out = returned(out)
     return out.reshape(query.shape)
 
 

time: 91.8 us -> 90.1 us (0.981)
  blocking collectives: 29.8 us -> 11 us
  starting transfers between devices: 38.5 us -> 48.8 us
  waiting for transfers between devices: 11.4 us -> 16.5 us
  Pallas kernels: 9.74 us -> 11.7 us
    all_to_all x2 -> x1, blocking collectives: 29.8 us -> 11 us  [exchange(): return lax.all_to_all(x, 'head', split_axis=0, concat_axis=0, tiled=True)]
    ppermute x0 -> x4, starting transfers between devices: none -> 10.3 us  [the longest x1 5.73 us: returned(): other = lax.ppermute(other, 'head', [(h, h ^ 1) for h in range(heads)])]
    ppermute x0 -> x4, waiting for transfers between devices: none -> 6.04 us  [the longest x3 4.88 us: returned(): lax.ppermute(pairs[to - 1], 'head', [(h, (h + 2 * to) % heads) for h in r...]
    pallas_call x5, Pallas kernels: 6.24 us -> 7.24 us  [run(): pl.pallas_call(functools.partial(attend, steps, refs, first, last), out_s...]
    ppermute x15, waiting for transfers between devices: 11.4 us -> 10.4 us  [shift(): return lax.ppermute(x, axis, [(i, (i + by) % size) for i in range(size)])]
    pallas_call x5 -> x7, Pallas kernels: 2.58 us -> 3.52 us  [moved(): pl.pallas_call(body, out_shape=[jax.ShapeDtypeStruct(shape, jnp.bfloat16)...]
  transfers between devices with their start and end apart: 16 -> 20, of which waited for: 6 -> 9; matrix products, arithmetic and copies ran while one was open for 0% -> 0% of each run, Pallas kernels for 9% -> 10%
where the time goes in v2:
time: 90.1 us; the launch traced here: 89.3 us
  starting transfers between devices  48.8 us (54%)
  waiting for transfers between devices  16.5 us (18%)
  Pallas kernels  11.7 us (13%)
  blocking collectives  11 us (12%)
  local copies, waits for them, and re-layouts  0.97 us (1%)
    ppermute x15, starting transfers between devices, shift(): return lax.ppermute(x, axis, [(i, (i + by) % size) for i in range(size)])  34 us
    all_to_all x1, blocking collectives, exchange(): return lax.all_to_all(x, 'head', split_axis=0, concat_axis=0, tiled=True)  11 us
    ppermute x15, waiting for transfers between devices, shift(): return lax.ppermute(x, axis, [(i, (i + by) % size) for i in range(size)])  10.4 us
    pallas_call x5, Pallas kernels, run(): pl.pallas_call(functools.partial(attend, steps, refs, first, last), out_s...  7.24 us
    ppermute x1, starting transfers between devices, returned(): other = lax.ppermute(other, 'head', [(h, h ^ 1) for h in range(heads)])  5.73 us
    ppermute x3, waiting for transfers between devices, returned(): lax.ppermute(pairs[to - 1], 'head', [(h, (h + 2 * to) % heads) for h in r...  4.88 us
    ppermute x3, starting transfers between devices, returned(): lax.ppermute(pairs[to - 1], 'head', [(h, (h + 2 * to) % heads) for h in r...  4.57 us
    all_to_all x1, starting transfers between devices, exchange(): return lax.all_to_all(x, 'head', split_axis=0, concat_axis=0, tiled=True)  4.54 us
  transfers between devices with their start and end apart: 20, of which 9 were waited for; matrix products, arithmetic and copies ran while one was open for 0% of the time, Pallas kernels for 10%

profile of v2, /device:TPU:1, one launch (start us, length us, event | category | flops | bytes accessed | tf_op | source)
XLA Modules:
  0.0 89.3 jit_solution(13492122541000197110)
XLA Ops:
  0.0 1.0 %copy-done.1 = bf16[1,2,2,16,1024]{4,3,2,1,0:T(8,128)(2,1)S(1)} copy-done((bf16[1,2,2,16,1024]{4,3,2,1,0:T(8,128)(2,1)S(1)}, bf16[1,2,2,16,1024]{4,3,2,1,0:T(8,128)(2,1)}, u32[]{:S(2)}) %copy-start.1) | copy-done | bytes 131096
  1.0 11.0 %all_to_all.10.in_ref = bf16[8,4,16,128]{3,2,1,0:T(8,128)(2,1)S(1)} all-to-all(bf16[8,4,16,128]{3,2,1,0:T(8,128)(2,1)S(1)} %shard_map.37), channel_id=1, replica_groups=mesh['z'=8,'x'=4,'head'=8] {'head'}, dimensions={0} | all-to-all | bytes 262144 | tf_op jit(solution)/shard_map/all_to_all | solution.py:269
  12.0 2.6 %collective-permute-start.1 = (bf16[1,4,128,128]{3,2,1,0:T(8,128)(2,1)S(1)}, bf16[1,4,128,128]{3,2,1,0:T(8,128)(2,1)S(1)}, u32[]{:S(2)}, u32[]{:S(2)}) collective-permute-start(bf16[1,4,128,128]{3,2,1,0:T(8,128)(2,1)S(1)} %shard_map.38.refs_0_), channel_id=1, source_target_pairs={{0,24},{8,0},{16,8},{24,16},{1,25},{9,1},{17,9},{25,17},{2,26},{10... | collective-permute-start | bytes 393224 | tf_op jit(solution)/shard_map/ppermute | solution.py:218
  14.6 0.0 collective-permute-start
  14.6 0.9 shard_map.40
  15.5 4.5 %all-to-all-start.1 = ((bf16[8,16,16,128]{3,2,1,0:T(8,128)(2,1)}), bf16[8,16,16,128]{3,2,1,0:T(8,128)(2,1)S(1)}, u32[]{:S(2)}, u32[]{:S(2)}) async-start(bf16[8,16,16,128]{3,2,1,0:T(8,128)(2,1)} %shard_map.40), calls=%async_computation.1 | async-start | bytes 1048576 | tf_op jit(solution)/shard_map/all_to_all | solution.py:269
  20.0 0.0 collective-permute-done.1.refs_2_
  20.0 0.0 collective-permute-done.refs_1_
  20.0 0.5 shard_map.39.refs_0_
  20.6 0.0 copy-start.2
  20.6 5.7 %collective-permute-start.3 = (bf16[3,4,128,128]{3,2,1,0:T(8,128)(2,1)S(1)}, bf16[3,4,128,128]{3,2,1,0:T(8,128)(2,1)S(1)}, u32[]{:S(2)}, u32[]{:S(2)}) collective-permute-start(bf16[3,4,128,128]{3,2,1,0:T(8,128)(2,1)S(1)} %shard_map.39.refs_0_), channel_id=1, source_target_pairs={{0,224},{32,0},{64,32},{96,64},{128,96},{160,128},{192,160},{224,1... | collective-permute-start | bytes 1179656 | tf_op jit(solution)/shard_map/ppermute | solution.py:218
  26.3 0.0 collective-permute-start.2
  26.3 2.0 %collective-permute-start.4 = (bf16[1,4,128,128]{3,2,1,0:T(8,128)(2,1)S(1)}, bf16[1,4,128,128]{3,2,1,0:T(8,128)(2,1)S(1)}, u32[]{:S(2)}, u32[]{:S(2)}) collective-permute-start(bf16[1,4,128,128]{3,2,1,0:T(8,128)(2,1)S(1)} %shard_map.38.refs_0_), channel_id=1, source_target_pairs={{0,16},{8,24},{16,0},{24,8},{1,17},{9,25},{17,1},{25,9},{2,18},{10... | collective-permute-start | bytes 393224 | tf_op jit(solution)/shard_map/ppermute | solution.py:218
  28.3 3.3 %collective-permute-done.4.refs_1_ = bf16[1,4,128,128]{3,2,1,0:T(8,128)(2,1)S(1)} collective-permute-done((bf16[1,4,128,128]{3,2,1,0:T(8,128)(2,1)S(1)}, bf16[1,4,128,128]{3,2,1,0:T(8,128)(2,1)S(1)}, u32[]{:S(2)}, u32[]{:S(2)}) %collective-permute-start.4) | collective-permute-done | bytes 131104 | tf_op jit(solution)/shard_map/ppermute | solution.py:218
  31.6 1.2 %collective-permute-done.3.refs_1_ = bf16[3,4,128,128]{3,2,1,0:T(8,128)(2,1)S(1)} collective-permute-done((bf16[3,4,128,128]{3,2,1,0:T(8,128)(2,1)S(1)}, bf16[3,4,128,128]{3,2,1,0:T(8,128)(2,1)S(1)}, u32[]{:S(2)}, u32[]{:S(2)}) %collective-permute-start.3) | collective-permute-done | bytes 393248 | tf_op jit(solution)/shard_map/ppermute | solution.py:218
  32.8 3.1 %collective-permute-done.2.refs_0_ = bf16[3,4,128,128]{3,2,1,0:T(8,128)(2,1)S(1)} collective-permute-done((bf16[3,4,128,128]{3,2,1,0:T(8,128)(2,1)S(1)}, bf16[3,4,128,128]{3,2,1,0:T(8,128)(2,1)S(1)}, u32[]{:S(2)}, u32[]{:S(2)}) %collective-permute-start.2) | collective-permute-done | bytes 393248 | tf_op jit(solution)/shard_map/ppermute | solution.py:218
  35.9 0.0 collective-permute-start.5
  35.9 2.7 %collective-permute-start.6 = (bf16[3,4,128,128]{3,2,1,0:T(8,128)(2,1)S(1)}, bf16[3,4,128,128]{3,2,1,0:T(8,128)(2,1)S(1)}, u32[]{:S(2)}, u32[]{:S(2)}) collective-permute-start(bf16[3,4,128,128]{3,2,1,0:T(8,128)(2,1)S(1)} %collective-permute-done.3.refs_1_), channel_id=1, source_target_pairs={{0,224},{32,0},{64,32},{96,64},{128,96},{160,128},{192,160},{224,1... | collective-permute-start | bytes 1179656 | tf_op jit(solution)/shard_map/ppermute | solution.py:218
  38.6 0.3 shard_map.42
  39.0 4.8 %collective-permute-start.9 = (bf16[2,4,128,128]{3,2,1,0:T(8,128)(2,1)S(1)}, bf16[2,4,128,128]{3,2,1,0:T(8,128)(2,1)S(1)}, u32[]{:S(2)}, u32[]{:S(2)}) collective-permute-start(bf16[2,4,128,128]{3,2,1,0:T(8,128)(2,1)S(1)} %shard_map.42), channel_id=1, source_target_pairs={{0,24},{8,0},{16,8},{24,16},{1,25},{9,1},{17,9},{25,17},{2,26},{10... | collective-permute-start | bytes 786440 | tf_op jit(solution)/shard_map/ppermute | solution.py:218
  43.8 3.0 %shard_map.41 = (f32[2,8,128,128]{3,2,1,0:T(8,128)S(1)}, f32[2,8,128,128]{3,2,1,0:T(8,128)S(1)}, f32[2,8,128,128]{3,2,1,0:T(8,128)S(1)}, bf16[2,8,128,128]{3,2,1,0:T(8,128)(2,1)S(1)}) custom-call(s32[4]{0:T(128)S(1)} %copy-done.2, bf16[8,16,16,128]{3,2,1,0:T(8,128)(2,1)S(1)} %all-to-all-done.1.rows_ref, bf16[3,4,128,128]{3,2,1,0:T(8,128)(2,1)S(1)} %shard_map.39.refs_0_, ...), custom_call_target="tpu_custom_call" | custom-call | flops 1073741824 | bytes 4194304 | tf_op jit(solution)/shard_map/pallas_call | solution.py:148
  46.7 0.0 collective-permute-done.6.refs_1_
  46.8 0.1 collective-permute-start.7
  46.8 2.7 %collective-permute-start.8 = (bf16[3,4,128,128]{3,2,1,0:T(8,128)(2,1)S(1)}, bf16[3,4,128,128]{3,2,1,0:T(8,128)(2,1)S(1)}, u32[]{:S(2)}, u32[]{:S(2)}) collective-permute-start(bf16[3,4,128,128]{3,2,1,0:T(8,128)(2,1)S(1)} %collective-permute-done.6.refs_1_), channel_id=1, source_target_pairs={{0,224},{32,0},{64,32},{96,64},{128,96},{160,128},{192,160},{224,1... | collective-permute-start | bytes 1179656 | tf_op jit(solution)/shard_map/ppermute | solution.py:218
  49.5 0.3 shard_map.45
  49.8 4.7 %collective-permute-start.12 = (bf16[2,4,128,128]{3,2,1,0:T(8,128)(2,1)S(1)}, bf16[2,4,128,128]{3,2,1,0:T(8,128)(2,1)S(1)}, u32[]{:S(2)}, u32[]{:S(2)}) collective-permute-start(bf16[2,4,128,128]{3,2,1,0:T(8,128)(2,1)S(1)} %shard_map.45), channel_id=1, source_target_pairs={{0,24},{8,0},{16,8},{24,16},{1,25},{9,1},{17,9},{25,17},{2,26},{10... | collective-permute-start | bytes 786440 | tf_op jit(solution)/shard_map/ppermute | solution.py:218
  54.5 1.8 %shard_map.43 = (f32[2,8,128,128]{3,2,1,0:T(8,128)S(1)}, f32[2,8,128,128]{3,2,1,0:T(8,128)S(1)}, f32[2,8,128,128]{3,2,1,0:T(8,128)S(1)}) custom-call(s32[4]{0:T(128)S(1)} %copy-done.2, bf16[2,8,128,128]{3,2,1,0:T(8,128)(2,1)S(1)} %get-tuple-element.46.rows_ref, ...), custom_call_target="tpu_custom_call", output_to_operand_aliasing={{0}: (5, {}), {1}: (6, {}), {2}: (7, {})} | custom-call | flops 2147483648 | bytes 4194304 | tf_op jit(solution)/shard_map/pallas_call | solution.py:148
  56.3 0.2 collective-permute-done.7.refs_0_
  56.6 0.5 shard_map.44
  57.1 0.1 collective-permute-start.10
  57.2 4.4 %collective-permute-start.14 = (bf16[2,4,128,128]{3,2,1,0:T(8,128)(2,1)S(1)}, bf16[2,4,128,128]{3,2,1,0:T(8,128)(2,1)S(1)}, u32[]{:S(2)}, u32[]{:S(2)}) collective-permute-start(bf16[2,4,128,128]{3,2,1,0:T(8,128)(2,1)S(1)} %get-tuple-element.72), channel_id=1, source_target_pairs={{0,24},{8,0},{16,8},{24,16},{1,25},{9,1},{17,9},{25,17},{2,26},{10... | collective-permute-start | bytes 786440 | tf_op jit(solution)/shard_map/ppermute | solution.py:218
  61.6 2.6 %collective-permute-start.11 = (bf16[1,4,128,128]{3,2,1,0:T(8,128)(2,1)S(1)}, bf16[1,4,128,128]{3,2,1,0:T(8,128)(2,1)S(1)}, u32[]{:S(2)}, u32[]{:S(2)}) collective-permute-start(bf16[1,4,128,128]{3,2,1,0:T(8,128)(2,1)S(1)} %get-tuple-element.63), channel_id=1, source_target_pairs={{0,224},{32,0},{64,32},{96,64},{128,96},{160,128},{192,160},{224,1... | collective-permute-start | bytes 393224 | tf_op jit(solution)/shard_map/ppermute | solution.py:218
  64.2 0.8 shard_map.46
  65.0 1.2 %collective-permute-done.11.refs_1_ = bf16[1,4,128,128]{3,2,1,0:T(8,128)(2,1)S(1)} collective-permute-done((bf16[1,4,128,128]{3,2,1,0:T(8,128)(2,1)S(1)}, bf16[1,4,128,128]{3,2,1,0:T(8,128)(2,1)S(1)}, u32[]{:S(2)}, u32[]{:S(2)}) %collective-permute-start.11) | collective-permute-done | bytes 131104 | tf_op jit(solution)/shard_map/ppermute | solution.py:218
  66.1 1.8 %collective-permute-start.13 = (bf16[1,4,128,128]{3,2,1,0:T(8,128)(2,1)S(1)}, bf16[1,4,128,128]{3,2,1,0:T(8,128)(2,1)S(1)}, u32[]{:S(2)}, u32[]{:S(2)}) collective-permute-start(bf16[1,4,128,128]{3,2,1,0:T(8,128)(2,1)S(1)} %collective-permute-done.11.refs_1_), channel_id=1, source_target_pairs={{0,24},{8,0},{16,8},{24,16},{1,25},{9,1},{17,9},{25,17},{2,26},{10... | collective-permute-start | bytes 393224 | tf_op jit(solution)/shard_map/ppermute | solution.py:218
  67.9 0.8 shard_map.47
  68.7 1.3 %collective-permute-done.13.refs_2_ = bf16[1,4,128,128]{3,2,1,0:T(8,128)(2,1)S(1)} collective-permute-done((bf16[1,4,128,128]{3,2,1,0:T(8,128)(2,1)S(1)}, bf16[1,4,128,128]{3,2,1,0:T(8,128)(2,1)S(1)}, u32[]{:S(2)}, u32[]{:S(2)}) %collective-permute-start.13) | collective-permute-done | bytes 131104 | tf_op jit(solution)/shard_map/ppermute | solution.py:218
  70.0 1.0 %shard_map.48 = (bf16[8,2,16,1024]{3,2,1,0:T(8,128)(2,1)S(1)}, f32[2,8,128,128]{3,2,1,0:T(8,128)S(1)}, f32[2,8,128,128]{3,2,1,0:T(8,128)S(1)}, f32[2,8,128,128]{3,2,1,0:T(8,128)S(1)}) custom-call(s32[4]{0:T(128)S(1)} %copy-done.2, ...), custom_call_target="tpu_custom_call", output_to_operand_aliasing={{1}: (5, {}), {2}: (6, {}), {3}: (7, {})} | custom-call | flops 1073741824 | bytes 4194304 | tf_op jit(solution)/shard_map/pallas_call | solution.py:148
  71.0 0.4 shard_map.49
  71.4 5.7 %collective-permute-start.15 = (bf16[4,2,16,1024]{3,2,1,0:T(8,128)(2,1)S(1)}, bf16[4,2,16,1024]{3,2,1,0:T(8,128)(2,1)S(1)}, u32[]{:S(2)}, u32[]{:S(2)}) collective-permute-start(bf16[4,2,16,1024]{3,2,1,0:T(8,128)(2,1)S(1)} %shard_map.49), channel_id=1, source_target_pairs={{0,1},{1,0},{2,3},{3,2},{4,5},{5,4},{6,7},{7,6},{8,9},{9,8},{10,11... | collective-permute-start | bytes 786440 | tf_op jit(solution)/shard_map/ppermute | solution.py:233
  77.1 1.2 %collective-permute-done.15.refs_1_ = bf16[4,2,16,1024]{3,2,1,0:T(8,128)(2,1)S(1)} collective-permute-done((bf16[4,2,16,1024]{3,2,1,0:T(8,128)(2,1)S(1)}, bf16[4,2,16,1024]{3,2,1,0:T(8,128)(2,1)S(1)}, u32[]{:S(2)}, u32[]{:S(2)}) %collective-permute-start.15) | collective-permute-done | bytes 262176 | tf_op jit(solution)/shard_map/ppermute | solution.py:233
  78.3 0.5 shard_map.50
  78.8 1.0 %collective-permute-start.16 = (bf16[2,2,16,1024]{3,2,1,0:T(8,128)(2,1)S(1)}, bf16[2,2,16,1024]{3,2,1,0:T(8,128)(2,1)S(1)}, u32[]{:S(2)}, u32[]{:S(2)}) collective-permute-start(bf16[2,2,16,1024]{3,2,1,0:T(8,128)(2,1)S(1)} %get-tuple-element.80), channel_id=1, source_target_pairs={{0,2},{1,3},{2,4},{3,5},{4,6},{5,7},{6,0},{7,1},{8,10},{9,11},{10,... | collective-permute-start | bytes 393224 | tf_op jit(solution)/shard_map/ppermute | solution.py:244
  79.8 2.4 %collective-permute-start.17 = (bf16[2,2,16,1024]{3,2,1,0:T(8,128)(2,1)S(1)}, bf16[2,2,16,1024]{3,2,1,0:T(8,128)(2,1)S(1)}, u32[]{:S(2)}, u32[]{:S(2)}) collective-permute-start(bf16[2,2,16,1024]{3,2,1,0:T(8,128)(2,1)S(1)} %get-tuple-element.81), channel_id=1, source_target_pairs={{0,4},{1,5},{2,6},{3,7},{4,0},{5,1},{6,2},{7,3},{8,12},{9,13},{10,... | collective-permute-start | bytes 393224 | tf_op jit(solution)/shard_map/ppermute | solution.py:244
  82.2 1.2 %collective-permute-start.18 = (bf16[2,2,16,1024]{3,2,1,0:T(8,128)(2,1)S(1)}, bf16[2,2,16,1024]{3,2,1,0:T(8,128)(2,1)S(1)}, u32[]{:S(2)}, u32[]{:S(2)}) collective-permute-start(bf16[2,2,16,1024]{3,2,1,0:T(8,128)(2,1)S(1)} %get-tuple-element.82), channel_id=1, source_target_pairs={{0,6},{1,7},{2,0},{3,1},{4,2},{5,3},{6,4},{7,5},{8,14},{9,15},{10,... | collective-permute-start | bytes 393224 | tf_op jit(solution)/shard_map/ppermute | solution.py:244
  83.4 1.4 %collective-permute-done.16.refs_2_ = bf16[2,2,16,1024]{3,2,1,0:T(8,128)(2,1)S(1)} collective-permute-done((bf16[2,2,16,1024]{3,2,1,0:T(8,128)(2,1)S(1)}, bf16[2,2,16,1024]{3,2,1,0:T(8,128)(2,1)S(1)}, u32[]{:S(2)}, u32[]{:S(2)}) %collective-permute-start.16) | collective-permute-done | bytes 131104 | tf_op jit(solution)/shard_map/ppermute | solution.py:244
  84.8 3.5 %collective-permute-done.17.refs_3_ = bf16[2,2,16,1024]{3,2,1,0:T(8,128)(2,1)S(1)} collective-permute-done((bf16[2,2,16,1024]{3,2,1,0:T(8,128)(2,1)S(1)}, bf16[2,2,16,1024]{3,2,1,0:T(8,128)(2,1)S(1)}, u32[]{:S(2)}, u32[]{:S(2)}) %collective-permute-start.17) | collective-permute-done | bytes 131104 | tf_op jit(solution)/shard_map/ppermute | solution.py:244
  88.3 0.8 shard_map.51
  (14 shorter events, 0.1 us)
Async XLA Ops:
  0.0 14.6 %copy-start = (bf16[1,2,16,8192]{3,2,1,0:T(8,128)(2,1)S(1)}, bf16[1,2,16,8192]{3,2,1,0:T(8,128)(2,1)}, u32[]{:S(2)}) copy-start(bf16[1,2,16,8192]{3,2,1,0:T(8,128)(2,1)} %param.3) | copy-start | bytes 1572868
  0.0 1.0 %copy-start.1 = (bf16[1,2,2,16,1024]{4,3,2,1,0:T(8,128)(2,1)S(1)}, bf16[1,2,2,16,1024]{4,3,2,1,0:T(8,128)(2,1)}, u32[]{:S(2)}) copy-start(bf16[1,2,2,16,1024]{4,3,2,1,0:T(8,128)(2,1)} %param.4) | copy-start | bytes 393220
  12.0 8.0 %collective-permute-start.1 = (bf16[1,4,128,128]{3,2,1,0:T(8,128)(2,1)S(1)}, bf16[1,4,128,128]{3,2,1,0:T(8,128)(2,1)S(1)}, u32[]{:S(2)}, u32[]{:S(2)}) collective-permute-start(bf16[1,4,128,128]{3,2,1,0:T(8,128)(2,1)S(1)} %shard_map.38.refs_0_), channel_id=1, source_target_pairs={{0,24},{8,0},{16,8},{24,16},{1,25},{9,1},{17,9},{25,17},{2,26},{10... | collective-permute-start | bytes 393224 | tf_op jit(solution)/shard_map/ppermute | solution.py:218
  14.6 5.4 %collective-permute-start = (bf16[1,4,128,128]{3,2,1,0:T(8,128)(2,1)S(1)}, bf16[1,4,128,128]{3,2,1,0:T(8,128)(2,1)S(1)}, u32[]{:S(2)}, u32[]{:S(2)}) collective-permute-start(bf16[1,4,128,128]{3,2,1,0:T(8,128)(2,1)S(1)} %shard_map.38.refs_0_), channel_id=1, source_target_pairs={{0,8},{8,16},{16,24},{24,0},{1,9},{9,17},{17,25},{25,1},{2,10},{10... | collective-permute-start | bytes 393224 | tf_op jit(solution)/shard_map/ppermute | solution.py:218
  15.5 16.1 %all-to-all-start.1 = ((bf16[8,16,16,128]{3,2,1,0:T(8,128)(2,1)}), bf16[8,16,16,128]{3,2,1,0:T(8,128)(2,1)S(1)}, u32[]{:S(2)}, u32[]{:S(2)}) async-start(bf16[8,16,16,128]{3,2,1,0:T(8,128)(2,1)} %shard_map.40), calls=%async_computation.1 | async-start | bytes 1048576 | tf_op jit(solution)/shard_map/all_to_all | solution.py:269
  20.6 23.2 %copy-start.2 = (s32[4]{0:T(128)S(1)}, s32[4]{0:T(128)}, u32[]{:S(2)}) copy-start(s32[4]{0:T(128)} %docs_ref.9) | copy-start | bytes 52
  20.6 12.2 %collective-permute-start.3 = (bf16[3,4,128,128]{3,2,1,0:T(8,128)(2,1)S(1)}, bf16[3,4,128,128]{3,2,1,0:T(8,128)(2,1)S(1)}, u32[]{:S(2)}, u32[]{:S(2)}) collective-permute-start(bf16[3,4,128,128]{3,2,1,0:T(8,128)(2,1)S(1)} %shard_map.39.refs_0_), channel_id=1, source_target_pairs={{0,224},{32,0},{64,32},{96,64},{128,96},{160,128},{192,160},{224,1... | collective-permute-start | bytes 1179656 | tf_op jit(solution)/shard_map/ppermute | solution.py:218
  26.3 9.7 %collective-permute-start.2 = (bf16[3,4,128,128]{3,2,1,0:T(8,128)(2,1)S(1)}, bf16[3,4,128,128]{3,2,1,0:T(8,128)(2,1)S(1)}, u32[]{:S(2)}, u32[]{:S(2)}) collective-permute-start(bf16[3,4,128,128]{3,2,1,0:T(8,128)(2,1)S(1)} %shard_map.39.refs_0_), channel_id=1, source_target_pairs={{0,32},{32,64},{64,96},{96,128},{128,160},{160,192},{192,224},{224... | collective-permute-start | bytes 1179656 | tf_op jit(solution)/shard_map/ppermute | solution.py:218
  26.3 5.3 %collective-permute-start.4 = (bf16[1,4,128,128]{3,2,1,0:T(8,128)(2,1)S(1)}, bf16[1,4,128,128]{3,2,1,0:T(8,128)(2,1)S(1)}, u32[]{:S(2)}, u32[]{:S(2)}) collective-permute-start(bf16[1,4,128,128]{3,2,1,0:T(8,128)(2,1)S(1)} %shard_map.38.refs_0_), channel_id=1, source_target_pairs={{0,16},{8,24},{16,0},{24,8},{1,17},{9,25},{17,1},{25,9},{2,18},{10... | collective-permute-start | bytes 393224 | tf_op jit(solution)/shard_map/ppermute | solution.py:218
  35.9 10.8 %collective-permute-start.5 = (bf16[3,4,128,128]{3,2,1,0:T(8,128)(2,1)S(1)}, bf16[3,4,128,128]{3,2,1,0:T(8,128)(2,1)S(1)}, u32[]{:S(2)}, u32[]{:S(2)}) collective-permute-start(bf16[3,4,128,128]{3,2,1,0:T(8,128)(2,1)S(1)} %collective-permute-done.2.refs_0_), channel_id=1, source_target_pairs={{0,32},{32,64},{64,96},{96,128},{128,160},{160,192},{192,224},{224... | collective-permute-start | bytes 1179656 | tf_op jit(solution)/shard_map/ppermute | solution.py:218
  35.9 10.8 %collective-permute-start.6 = (bf16[3,4,128,128]{3,2,1,0:T(8,128)(2,1)S(1)}, bf16[3,4,128,128]{3,2,1,0:T(8,128)(2,1)S(1)}, u32[]{:S(2)}, u32[]{:S(2)}) collective-permute-start(bf16[3,4,128,128]{3,2,1,0:T(8,128)(2,1)S(1)} %collective-permute-done.3.refs_1_), channel_id=1, source_target_pairs={{0,224},{32,0},{64,32},{96,64},{128,96},{160,128},{192,160},{224,1... | collective-permute-start | bytes 1179656 | tf_op jit(solution)/shard_map/ppermute | solution.py:218
  39.0 15.6 %collective-permute-start.9 = (bf16[2,4,128,128]{3,2,1,0:T(8,128)(2,1)S(1)}, bf16[2,4,128,128]{3,2,1,0:T(8,128)(2,1)S(1)}, u32[]{:S(2)}, u32[]{:S(2)}) collective-permute-start(bf16[2,4,128,128]{3,2,1,0:T(8,128)(2,1)S(1)} %shard_map.42), channel_id=1, source_target_pairs={{0,24},{8,0},{16,8},{24,16},{1,25},{9,1},{17,9},{25,17},{2,26},{10... | collective-permute-start | bytes 786440 | tf_op jit(solution)/shard_map/ppermute | solution.py:218
  46.8 9.8 %collective-permute-start.7 = (bf16[3,4,128,128]{3,2,1,0:T(8,128)(2,1)S(1)}, bf16[3,4,128,128]{3,2,1,0:T(8,128)(2,1)S(1)}, u32[]{:S(2)}, u32[]{:S(2)}) collective-permute-start(bf16[3,4,128,128]{3,2,1,0:T(8,128)(2,1)S(1)} %collective-permute-done.5.refs_0_), channel_id=1, source_target_pairs={{0,32},{32,64},{64,96},{96,128},{128,160},{160,192},{192,224},{224... | collective-permute-start | bytes 1179656 | tf_op jit(solution)/shard_map/ppermute | solution.py:218
  46.8 9.7 %collective-permute-start.8 = (bf16[3,4,128,128]{3,2,1,0:T(8,128)(2,1)S(1)}, bf16[3,4,128,128]{3,2,1,0:T(8,128)(2,1)S(1)}, u32[]{:S(2)}, u32[]{:S(2)}) collective-permute-start(bf16[3,4,128,128]{3,2,1,0:T(8,128)(2,1)S(1)} %collective-permute-done.6.refs_1_), channel_id=1, source_target_pairs={{0,224},{32,0},{64,32},{96,64},{128,96},{160,128},{192,160},{224,1... | collective-permute-start | bytes 1179656 | tf_op jit(solution)/shard_map/ppermute | solution.py:218
  49.8 14.3 %collective-permute-start.12 = (bf16[2,4,128,128]{3,2,1,0:T(8,128)(2,1)S(1)}, bf16[2,4,128,128]{3,2,1,0:T(8,128)(2,1)S(1)}, u32[]{:S(2)}, u32[]{:S(2)}) collective-permute-start(bf16[2,4,128,128]{3,2,1,0:T(8,128)(2,1)S(1)} %shard_map.45), channel_id=1, source_target_pairs={{0,24},{8,0},{16,8},{24,16},{1,25},{9,1},{17,9},{25,17},{2,26},{10... | collective-permute-start | bytes 786440 | tf_op jit(solution)/shard_map/ppermute | solution.py:218
  57.1 9.0 %collective-permute-start.10 = (bf16[2,4,128,128]{3,2,1,0:T(8,128)(2,1)S(1)}, bf16[2,4,128,128]{3,2,1,0:T(8,128)(2,1)S(1)}, u32[]{:S(2)}, u32[]{:S(2)}) collective-permute-start(bf16[2,4,128,128]{3,2,1,0:T(8,128)(2,1)S(1)} %get-tuple-element.62), channel_id=1, source_target_pairs={{0,32},{32,64},{64,96},{96,128},{128,160},{160,192},{192,224},{224... | collective-permute-start | bytes 786440 | tf_op jit(solution)/shard_map/ppermute | solution.py:218
  57.2 10.7 %collective-permute-start.14 = (bf16[2,4,128,128]{3,2,1,0:T(8,128)(2,1)S(1)}, bf16[2,4,128,128]{3,2,1,0:T(8,128)(2,1)S(1)}, u32[]{:S(2)}, u32[]{:S(2)}) collective-permute-start(bf16[2,4,128,128]{3,2,1,0:T(8,128)(2,1)S(1)} %get-tuple-element.72), channel_id=1, source_target_pairs={{0,24},{8,0},{16,8},{24,16},{1,25},{9,1},{17,9},{25,17},{2,26},{10... | collective-permute-start | bytes 786440 | tf_op jit(solution)/shard_map/ppermute | solution.py:218
  61.6 4.5 %collective-permute-start.11 = (bf16[1,4,128,128]{3,2,1,0:T(8,128)(2,1)S(1)}, bf16[1,4,128,128]{3,2,1,0:T(8,128)(2,1)S(1)}, u32[]{:S(2)}, u32[]{:S(2)}) collective-permute-start(bf16[1,4,128,128]{3,2,1,0:T(8,128)(2,1)S(1)} %get-tuple-element.63), channel_id=1, source_target_pairs={{0,224},{32,0},{64,32},{96,64},{128,96},{160,128},{192,160},{224,1... | collective-permute-start | bytes 393224 | tf_op jit(solution)/shard_map/ppermute | solution.py:218
  66.1 3.9 %collective-permute-start.13 = (bf16[1,4,128,128]{3,2,1,0:T(8,128)(2,1)S(1)}, bf16[1,4,128,128]{3,2,1,0:T(8,128)(2,1)S(1)}, u32[]{:S(2)}, u32[]{:S(2)}) collective-permute-start(bf16[1,4,128,128]{3,2,1,0:T(8,128)(2,1)S(1)} %collective-permute-done.11.refs_1_), channel_id=1, source_target_pairs={{0,24},{8,0},{16,8},{24,16},{1,25},{9,1},{17,9},{25,17},{2,26},{10... | collective-permute-start | bytes 393224 | tf_op jit(solution)/shard_map/ppermute | solution.py:218
  71.4 6.9 %collective-permute-start.15 = (bf16[4,2,16,1024]{3,2,1,0:T(8,128)(2,1)S(1)}, bf16[4,2,16,1024]{3,2,1,0:T(8,128)(2,1)S(1)}, u32[]{:S(2)}, u32[]{:S(2)}) collective-permute-start(bf16[4,2,16,1024]{3,2,1,0:T(8,128)(2,1)S(1)} %shard_map.49), channel_id=1, source_target_pairs={{0,1},{1,0},{2,3},{3,2},{4,5},{5,4},{6,7},{7,6},{8,9},{9,8},{10,11... | collective-permute-start | bytes 786440 | tf_op jit(solution)/shard_map/ppermute | solution.py:233
  78.8 6.0 %collective-permute-start.16 = (bf16[2,2,16,1024]{3,2,1,0:T(8,128)(2,1)S(1)}, bf16[2,2,16,1024]{3,2,1,0:T(8,128)(2,1)S(1)}, u32[]{:S(2)}, u32[]{:S(2)}) collective-permute-start(bf16[2,2,16,1024]{3,2,1,0:T(8,128)(2,1)S(1)} %get-tuple-element.80), channel_id=1, source_target_pairs={{0,2},{1,3},{2,4},{3,5},{4,6},{5,7},{6,0},{7,1},{8,10},{9,11},{10,... | collective-permute-start | bytes 393224 | tf_op jit(solution)/shard_map/ppermute | solution.py:244
  79.8 8.5 %collective-permute-start.17 = (bf16[2,2,16,1024]{3,2,1,0:T(8,128)(2,1)S(1)}, bf16[2,2,16,1024]{3,2,1,0:T(8,128)(2,1)S(1)}, u32[]{:S(2)}, u32[]{:S(2)}) collective-permute-start(bf16[2,2,16,1024]{3,2,1,0:T(8,128)(2,1)S(1)} %get-tuple-element.81), channel_id=1, source_target_pairs={{0,4},{1,5},{2,6},{3,7},{4,0},{5,1},{6,2},{7,3},{8,12},{9,13},{10,... | collective-permute-start | bytes 393224 | tf_op jit(solution)/shard_map/ppermute | solution.py:244
  82.2 6.1 %collective-permute-start.18 = (bf16[2,2,16,1024]{3,2,1,0:T(8,128)(2,1)S(1)}, bf16[2,2,16,1024]{3,2,1,0:T(8,128)(2,1)S(1)}, u32[]{:S(2)}, u32[]{:S(2)}) collective-permute-start(bf16[2,2,16,1024]{3,2,1,0:T(8,128)(2,1)S(1)} %get-tuple-element.82), channel_id=1, source_target_pairs={{0,6},{1,7},{2,0},{3,1},{4,2},{5,3},{6,4},{7,5},{8,14},{9,15},{10,... | collective-permute-start | bytes 393224 | tf_op jit(solution)/shard_map/ppermute | solution.py:244

commit v3 on v2

--- a/solution.py
+++ b/solution.py
@@ -17,7 +17,7 @@
 SPAN_COUNT = 2 * Z * X
 CTX = ("z", "x")
 FAR = -1e30
-WIDE = 2
+WIDE = 4
 ORDER = (0, 1, 3, 2)
 SCALE = HEAD_WIDTH ** (-0.5) * 1.4426950408889634
 
@@ -301,7 +301,8 @@
                 [up, down],
                 [(2, *block), (2, *block), (1, *block)],
             )
-        following = shift(ahead, "z", Z, 1), shift(behind, "z", Z, -1)
+        back = shift(behind, "z", Z, -1)
+        following = shift(ahead, "z", Z, 1), back
         cross = shift(cross, "x", X, -1)
         picks = [[(side, 0), (side, 1), (side, 2), (2, side)] for side in range(2)]
         steps = [(-k, picks[0]), (k, picks[1])]

time: 90.1 us -> 91 us (level)
  Pallas kernels: 11.7 us -> 10.6 us
  waiting for transfers between devices: 16.5 us -> 17.5 us
    pallas_call x5, Pallas kernels: 7.24 us -> 6.21 us  [run(): pl.pallas_call(functools.partial(attend, steps, refs, first, last), out_s...]
    ppermute x15, waiting for transfers between devices: 10.4 us -> 11.4 us  [shift(): return lax.ppermute(x, axis, [(i, (i + by) % size) for i in range(size)])]
  transfers between devices with their start and end apart: 20 -> 20, of which waited for: 9 -> 9; matrix products, arithmetic and copies ran while one was open for 0% -> 0% of each run, Pallas kernels for 10% -> 9%
where the time goes in v3:
time: 91 us; the launch traced here: 89.3 us
  starting transfers between devices  48.8 us (54%)
  waiting for transfers between devices  17.5 us (19%)
  blocking collectives  11 us (12%)
  Pallas kernels  10.6 us (12%)
  local copies, waits for them, and re-layouts  0.97 us (1%)
    ppermute x15, starting transfers between devices, shift(): return lax.ppermute(x, axis, [(i, (i + by) % size) for i in range(size)])  34 us
    ppermute x15, waiting for transfers between devices, shift(): return lax.ppermute(x, axis, [(i, (i + by) % size) for i in range(size)])  11.4 us
    all_to_all x1, blocking collectives, exchange(): return lax.all_to_all(x, 'head', split_axis=0, concat_axis=0, tiled=True)  11 us
    pallas_call x5, Pallas kernels, run(): pl.pallas_call(functools.partial(attend, steps, refs, first, last), out_s...  6.21 us
    ppermute x1, starting transfers between devices, returned(): other = lax.ppermute(other, 'head', [(h, h ^ 1) for h in range(heads)])  5.73 us
    ppermute x3, waiting for transfers between devices, returned(): lax.ppermute(pairs[to - 1], 'head', [(h, (h + 2 * to) % heads) for h in r...  4.88 us
    ppermute x3, starting transfers between devices, returned(): lax.ppermute(pairs[to - 1], 'head', [(h, (h + 2 * to) % heads) for h in r...  4.57 us
    all_to_all x1, starting transfers between devices, exchange(): return lax.all_to_all(x, 'head', split_axis=0, concat_axis=0, tiled=True)  4.54 us
  transfers between devices with their start and end apart: 20, of which 9 were waited for; matrix products, arithmetic and copies ran while one was open for 0% of the time, Pallas kernels for 9%

profile of v3, /device:TPU:1, one launch (start us, length us, event | category | flops | bytes accessed | tf_op | source)
XLA Modules:
  0.0 89.3 jit_solution(5770334710813090370)
XLA Ops:
  0.0 1.0 %copy-done.1 = bf16[1,2,2,16,1024]{4,3,2,1,0:T(8,128)(2,1)S(1)} copy-done((bf16[1,2,2,16,1024]{4,3,2,1,0:T(8,128)(2,1)S(1)}, bf16[1,2,2,16,1024]{4,3,2,1,0:T(8,128)(2,1)}, u32[]{:S(2)}) %copy-start.1) | copy-done | bytes 131096
  1.0 11.0 %all_to_all.10.in_ref = bf16[8,4,16,128]{3,2,1,0:T(8,128)(2,1)S(1)} all-to-all(bf16[8,4,16,128]{3,2,1,0:T(8,128)(2,1)S(1)} %shard_map.37), channel_id=1, replica_groups=mesh['z'=8,'x'=4,'head'=8] {'head'}, dimensions={0} | all-to-all | bytes 262144 | tf_op jit(solution)/shard_map/all_to_all | solution.py:269
  12.0 2.6 %collective-permute-start.1 = (bf16[1,4,128,128]{3,2,1,0:T(8,128)(2,1)S(1)}, bf16[1,4,128,128]{3,2,1,0:T(8,128)(2,1)S(1)}, u32[]{:S(2)}, u32[]{:S(2)}) collective-permute-start(bf16[1,4,128,128]{3,2,1,0:T(8,128)(2,1)S(1)} %shard_map.38.refs_0_), channel_id=1, source_target_pairs={{0,24},{8,0},{16,8},{24,16},{1,25},{9,1},{17,9},{25,17},{2,26},{10... | collective-permute-start | bytes 393224 | tf_op jit(solution)/shard_map/ppermute | solution.py:218
  14.6 0.0 collective-permute-start
  14.6 0.9 shard_map.40
  15.5 4.5 %all-to-all-start.1 = ((bf16[8,16,16,128]{3,2,1,0:T(8,128)(2,1)}), bf16[8,16,16,128]{3,2,1,0:T(8,128)(2,1)S(1)}, u32[]{:S(2)}, u32[]{:S(2)}) async-start(bf16[8,16,16,128]{3,2,1,0:T(8,128)(2,1)} %shard_map.40), calls=%async_computation.1 | async-start | bytes 1048576 | tf_op jit(solution)/shard_map/all_to_all | solution.py:269
  20.0 0.0 collective-permute-done.1.refs_2_
  20.0 0.5 shard_map.39.refs_0_
  20.6 0.0 copy-start.2
  20.6 5.7 %collective-permute-start.3 = (bf16[3,4,128,128]{3,2,1,0:T(8,128)(2,1)S(1)}, bf16[3,4,128,128]{3,2,1,0:T(8,128)(2,1)S(1)}, u32[]{:S(2)}, u32[]{:S(2)}) collective-permute-start(bf16[3,4,128,128]{3,2,1,0:T(8,128)(2,1)S(1)} %shard_map.39.refs_0_), channel_id=1, source_target_pairs={{0,224},{32,0},{64,32},{96,64},{128,96},{160,128},{192,160},{224,1... | collective-permute-start | bytes 1179656 | tf_op jit(solution)/shard_map/ppermute | solution.py:218
  26.3 2.0 %collective-permute-start.4 = (bf16[1,4,128,128]{3,2,1,0:T(8,128)(2,1)S(1)}, bf16[1,4,128,128]{3,2,1,0:T(8,128)(2,1)S(1)}, u32[]{:S(2)}, u32[]{:S(2)}) collective-permute-start(bf16[1,4,128,128]{3,2,1,0:T(8,128)(2,1)S(1)} %shard_map.38.refs_0_), channel_id=1, source_target_pairs={{0,16},{8,24},{16,0},{24,8},{1,17},{9,25},{17,1},{25,9},{2,18},{10... | collective-permute-start | bytes 393224 | tf_op jit(solution)/shard_map/ppermute | solution.py:218
  28.3 3.3 %collective-permute-done.4.refs_1_ = bf16[1,4,128,128]{3,2,1,0:T(8,128)(2,1)S(1)} collective-permute-done((bf16[1,4,128,128]{3,2,1,0:T(8,128)(2,1)S(1)}, bf16[1,4,128,128]{3,2,1,0:T(8,128)(2,1)S(1)}, u32[]{:S(2)}, u32[]{:S(2)}) %collective-permute-start.4) | collective-permute-done | bytes 131104 | tf_op jit(solution)/shard_map/ppermute | solution.py:218
  31.6 0.0 all-to-all-done.1.rows_ref
  31.6 1.2 %collective-permute-done.3.refs_1_ = bf16[3,4,128,128]{3,2,1,0:T(8,128)(2,1)S(1)} collective-permute-done((bf16[3,4,128,128]{3,2,1,0:T(8,128)(2,1)S(1)}, bf16[3,4,128,128]{3,2,1,0:T(8,128)(2,1)S(1)}, u32[]{:S(2)}, u32[]{:S(2)}) %collective-permute-start.3) | collective-permute-done | bytes 393248 | tf_op jit(solution)/shard_map/ppermute | solution.py:218
  32.8 3.1 %collective-permute-done.2.refs_0_ = bf16[3,4,128,128]{3,2,1,0:T(8,128)(2,1)S(1)} collective-permute-done((bf16[3,4,128,128]{3,2,1,0:T(8,128)(2,1)S(1)}, bf16[3,4,128,128]{3,2,1,0:T(8,128)(2,1)S(1)}, u32[]{:S(2)}, u32[]{:S(2)}) %collective-permute-start.2) | collective-permute-done | bytes 393248 | tf_op jit(solution)/shard_map/ppermute | solution.py:218
  35.9 0.0 collective-permute-start.5
  35.9 2.7 %collective-permute-start.6 = (bf16[3,4,128,128]{3,2,1,0:T(8,128)(2,1)S(1)}, bf16[3,4,128,128]{3,2,1,0:T(8,128)(2,1)S(1)}, u32[]{:S(2)}, u32[]{:S(2)}) collective-permute-start(bf16[3,4,128,128]{3,2,1,0:T(8,128)(2,1)S(1)} %collective-permute-done.3.refs_1_), channel_id=1, source_target_pairs={{0,224},{32,0},{64,32},{96,64},{128,96},{160,128},{192,160},{224,1... | collective-permute-start | bytes 1179656 | tf_op jit(solution)/shard_map/ppermute | solution.py:218
  38.6 0.3 shard_map.42
  39.0 4.8 %collective-permute-start.9 = (bf16[2,4,128,128]{3,2,1,0:T(8,128)(2,1)S(1)}, bf16[2,4,128,128]{3,2,1,0:T(8,128)(2,1)S(1)}, u32[]{:S(2)}, u32[]{:S(2)}) collective-permute-start(bf16[2,4,128,128]{3,2,1,0:T(8,128)(2,1)S(1)} %shard_map.42), channel_id=1, source_target_pairs={{0,24},{8,0},{16,8},{24,16},{1,25},{9,1},{17,9},{25,17},{2,26},{10... | collective-permute-start | bytes 786440 | tf_op jit(solution)/shard_map/ppermute | solution.py:218
  43.8 3.0 %shard_map.41 = (f32[2,8,128,128]{3,2,1,0:T(8,128)S(1)}, f32[2,8,128,128]{3,2,1,0:T(8,128)S(1)}, f32[2,8,128,128]{3,2,1,0:T(8,128)S(1)}, bf16[2,8,128,128]{3,2,1,0:T(8,128)(2,1)S(1)}) custom-call(s32[4]{0:T(128)S(1)} %copy-done.2, bf16[8,16,16,128]{3,2,1,0:T(8,128)(2,1)S(1)} %all-to-all-done.1.rows_ref, bf16[3,4,128,128]{3,2,1,0:T(8,128)(2,1)S(1)} %shard_map.39.refs_0_, ...), custom_call_target="tpu_custom_call" | custom-call | flops 1073741824 | bytes 4194304 | tf_op jit(solution)/shard_map/pallas_call | solution.py:148
  46.7 0.0 collective-permute-done.5.refs_0_
  46.8 0.1 collective-permute-start.7
  46.8 2.7 %collective-permute-start.8 = (bf16[3,4,128,128]{3,2,1,0:T(8,128)(2,1)S(1)}, bf16[3,4,128,128]{3,2,1,0:T(8,128)(2,1)S(1)}, u32[]{:S(2)}, u32[]{:S(2)}) collective-permute-start(bf16[3,4,128,128]{3,2,1,0:T(8,128)(2,1)S(1)} %collective-permute-done.6.refs_1_), channel_id=1, source_target_pairs={{0,224},{32,0},{64,32},{96,64},{128,96},{160,128},{192,160},{224,1... | collective-permute-start | bytes 1179656 | tf_op jit(solution)/shard_map/ppermute | solution.py:218
  49.5 0.3 shard_map.45
  49.8 4.7 %collective-permute-start.12 = (bf16[2,4,128,128]{3,2,1,0:T(8,128)(2,1)S(1)}, bf16[2,4,128,128]{3,2,1,0:T(8,128)(2,1)S(1)}, u32[]{:S(2)}, u32[]{:S(2)}) collective-permute-start(bf16[2,4,128,128]{3,2,1,0:T(8,128)(2,1)S(1)} %shard_map.45), channel_id=1, source_target_pairs={{0,24},{8,0},{16,8},{24,16},{1,25},{9,1},{17,9},{25,17},{2,26},{10... | collective-permute-start | bytes 786440 | tf_op jit(solution)/shard_map/ppermute | solution.py:218
  54.5 0.8 shard_map.43
  55.3 1.3 %collective-permute-done.7.refs_0_ = bf16[3,4,128,128]{3,2,1,0:T(8,128)(2,1)S(1)} collective-permute-done((bf16[3,4,128,128]{3,2,1,0:T(8,128)(2,1)S(1)}, bf16[3,4,128,128]{3,2,1,0:T(8,128)(2,1)S(1)}, u32[]{:S(2)}, u32[]{:S(2)}) %collective-permute-start.7) | collective-permute-done | bytes 393248 | tf_op jit(solution)/shard_map/ppermute | solution.py:218
  56.6 0.5 shard_map.44
  57.1 0.1 collective-permute-start.10
  57.2 4.4 %collective-permute-start.14 = (bf16[2,4,128,128]{3,2,1,0:T(8,128)(2,1)S(1)}, bf16[2,4,128,128]{3,2,1,0:T(8,128)(2,1)S(1)}, u32[]{:S(2)}, u32[]{:S(2)}) collective-permute-start(bf16[2,4,128,128]{3,2,1,0:T(8,128)(2,1)S(1)} %get-tuple-element.72), channel_id=1, source_target_pairs={{0,24},{8,0},{16,8},{24,16},{1,25},{9,1},{17,9},{25,17},{2,26},{10... | collective-permute-start | bytes 786440 | tf_op jit(solution)/shard_map/ppermute | solution.py:218
  61.6 2.6 %collective-permute-start.11 = (bf16[1,4,128,128]{3,2,1,0:T(8,128)(2,1)S(1)}, bf16[1,4,128,128]{3,2,1,0:T(8,128)(2,1)S(1)}, u32[]{:S(2)}, u32[]{:S(2)}) collective-permute-start(bf16[1,4,128,128]{3,2,1,0:T(8,128)(2,1)S(1)} %get-tuple-element.63), channel_id=1, source_target_pairs={{0,224},{32,0},{64,32},{96,64},{128,96},{160,128},{192,160},{224,1... | collective-permute-start | bytes 393224 | tf_op jit(solution)/shard_map/ppermute | solution.py:218
  64.2 0.8 shard_map.46
  65.0 1.2 %collective-permute-done.11.refs_1_ = bf16[1,4,128,128]{3,2,1,0:T(8,128)(2,1)S(1)} collective-permute-done((bf16[1,4,128,128]{3,2,1,0:T(8,128)(2,1)S(1)}, bf16[1,4,128,128]{3,2,1,0:T(8,128)(2,1)S(1)}, u32[]{:S(2)}, u32[]{:S(2)}) %collective-permute-start.11) | collective-permute-done | bytes 131104 | tf_op jit(solution)/shard_map/ppermute | solution.py:218
  66.1 1.8 %collective-permute-start.13 = (bf16[1,4,128,128]{3,2,1,0:T(8,128)(2,1)S(1)}, bf16[1,4,128,128]{3,2,1,0:T(8,128)(2,1)S(1)}, u32[]{:S(2)}, u32[]{:S(2)}) collective-permute-start(bf16[1,4,128,128]{3,2,1,0:T(8,128)(2,1)S(1)} %collective-permute-done.11.refs_1_), channel_id=1, source_target_pairs={{0,24},{8,0},{16,8},{24,16},{1,25},{9,1},{17,9},{25,17},{2,26},{10... | collective-permute-start | bytes 393224 | tf_op jit(solution)/shard_map/ppermute | solution.py:218
  67.9 0.8 shard_map.47
  68.7 1.3 %collective-permute-done.13.refs_2_ = bf16[1,4,128,128]{3,2,1,0:T(8,128)(2,1)S(1)} collective-permute-done((bf16[1,4,128,128]{3,2,1,0:T(8,128)(2,1)S(1)}, bf16[1,4,128,128]{3,2,1,0:T(8,128)(2,1)S(1)}, u32[]{:S(2)}, u32[]{:S(2)}) %collective-permute-start.13) | collective-permute-done | bytes 131104 | tf_op jit(solution)/shard_map/ppermute | solution.py:218
  70.0 1.0 %shard_map.48 = (bf16[8,2,16,1024]{3,2,1,0:T(8,128)(2,1)S(1)}, f32[2,8,128,128]{3,2,1,0:T(8,128)S(1)}, f32[2,8,128,128]{3,2,1,0:T(8,128)S(1)}, f32[2,8,128,128]{3,2,1,0:T(8,128)S(1)}) custom-call(s32[4]{0:T(128)S(1)} %copy-done.2, ...), custom_call_target="tpu_custom_call", output_to_operand_aliasing={{1}: (5, {}), {2}: (6, {}), {3}: (7, {})} | custom-call | flops 1073741824 | bytes 4194304 | tf_op jit(solution)/shard_map/pallas_call | solution.py:148
  71.0 0.4 shard_map.49
  71.4 5.7 %collective-permute-start.15 = (bf16[4,2,16,1024]{3,2,1,0:T(8,128)(2,1)S(1)}, bf16[4,2,16,1024]{3,2,1,0:T(8,128)(2,1)S(1)}, u32[]{:S(2)}, u32[]{:S(2)}) collective-permute-start(bf16[4,2,16,1024]{3,2,1,0:T(8,128)(2,1)S(1)} %shard_map.49), channel_id=1, source_target_pairs={{0,1},{1,0},{2,3},{3,2},{4,5},{5,4},{6,7},{7,6},{8,9},{9,8},{10,11... | collective-permute-start | bytes 786440 | tf_op jit(solution)/shard_map/ppermute | solution.py:233
  77.1 1.2 %collective-permute-done.15.refs_1_ = bf16[4,2,16,1024]{3,2,1,0:T(8,128)(2,1)S(1)} collective-permute-done((bf16[4,2,16,1024]{3,2,1,0:T(8,128)(2,1)S(1)}, bf16[4,2,16,1024]{3,2,1,0:T(8,128)(2,1)S(1)}, u32[]{:S(2)}, u32[]{:S(2)}) %collective-permute-start.15) | collective-permute-done | bytes 262176 | tf_op jit(solution)/shard_map/ppermute | solution.py:233
  78.3 0.5 shard_map.50
  78.8 1.0 %collective-permute-start.16 = (bf16[2,2,16,1024]{3,2,1,0:T(8,128)(2,1)S(1)}, bf16[2,2,16,1024]{3,2,1,0:T(8,128)(2,1)S(1)}, u32[]{:S(2)}, u32[]{:S(2)}) collective-permute-start(bf16[2,2,16,1024]{3,2,1,0:T(8,128)(2,1)S(1)} %get-tuple-element.80), channel_id=1, source_target_pairs={{0,2},{1,3},{2,4},{3,5},{4,6},{5,7},{6,0},{7,1},{8,10},{9,11},{10,... | collective-permute-start | bytes 393224 | tf_op jit(solution)/shard_map/ppermute | solution.py:244
  79.8 2.4 %collective-permute-start.17 = (bf16[2,2,16,1024]{3,2,1,0:T(8,128)(2,1)S(1)}, bf16[2,2,16,1024]{3,2,1,0:T(8,128)(2,1)S(1)}, u32[]{:S(2)}, u32[]{:S(2)}) collective-permute-start(bf16[2,2,16,1024]{3,2,1,0:T(8,128)(2,1)S(1)} %get-tuple-element.81), channel_id=1, source_target_pairs={{0,4},{1,5},{2,6},{3,7},{4,0},{5,1},{6,2},{7,3},{8,12},{9,13},{10,... | collective-permute-start | bytes 393224 | tf_op jit(solution)/shard_map/ppermute | solution.py:244
  82.2 1.2 %collective-permute-start.18 = (bf16[2,2,16,1024]{3,2,1,0:T(8,128)(2,1)S(1)}, bf16[2,2,16,1024]{3,2,1,0:T(8,128)(2,1)S(1)}, u32[]{:S(2)}, u32[]{:S(2)}) collective-permute-start(bf16[2,2,16,1024]{3,2,1,0:T(8,128)(2,1)S(1)} %get-tuple-element.82), channel_id=1, source_target_pairs={{0,6},{1,7},{2,0},{3,1},{4,2},{5,3},{6,4},{7,5},{8,14},{9,15},{10,... | collective-permute-start | bytes 393224 | tf_op jit(solution)/shard_map/ppermute | solution.py:244
  83.4 1.4 %collective-permute-done.16.refs_2_ = bf16[2,2,16,1024]{3,2,1,0:T(8,128)(2,1)S(1)} collective-permute-done((bf16[2,2,16,1024]{3,2,1,0:T(8,128)(2,1)S(1)}, bf16[2,2,16,1024]{3,2,1,0:T(8,128)(2,1)S(1)}, u32[]{:S(2)}, u32[]{:S(2)}) %collective-permute-start.16) | collective-permute-done | bytes 131104 | tf_op jit(solution)/shard_map/ppermute | solution.py:244
  84.8 3.5 %collective-permute-done.17.refs_3_ = bf16[2,2,16,1024]{3,2,1,0:T(8,128)(2,1)S(1)} collective-permute-done((bf16[2,2,16,1024]{3,2,1,0:T(8,128)(2,1)S(1)}, bf16[2,2,16,1024]{3,2,1,0:T(8,128)(2,1)S(1)}, u32[]{:S(2)}, u32[]{:S(2)}) %collective-permute-start.17) | collective-permute-done | bytes 131104 | tf_op jit(solution)/shard_map/ppermute | solution.py:244
  88.3 0.0 collective-permute-done.18.refs_4_
  88.3 0.8 shard_map.51
  (14 shorter events, 0.1 us)
Async XLA Ops:
  0.0 14.6 %copy-start = (bf16[1,2,16,8192]{3,2,1,0:T(8,128)(2,1)S(1)}, bf16[1,2,16,8192]{3,2,1,0:T(8,128)(2,1)}, u32[]{:S(2)}) copy-start(bf16[1,2,16,8192]{3,2,1,0:T(8,128)(2,1)} %param.3) | copy-start | bytes 1572868
  0.0 1.0 %copy-start.1 = (bf16[1,2,2,16,1024]{4,3,2,1,0:T(8,128)(2,1)S(1)}, bf16[1,2,2,16,1024]{4,3,2,1,0:T(8,128)(2,1)}, u32[]{:S(2)}) copy-start(bf16[1,2,2,16,1024]{4,3,2,1,0:T(8,128)(2,1)} %param.4) | copy-start | bytes 393220
  12.0 8.0 %collective-permute-start.1 = (bf16[1,4,128,128]{3,2,1,0:T(8,128)(2,1)S(1)}, bf16[1,4,128,128]{3,2,1,0:T(8,128)(2,1)S(1)}, u32[]{:S(2)}, u32[]{:S(2)}) collective-permute-start(bf16[1,4,128,128]{3,2,1,0:T(8,128)(2,1)S(1)} %shard_map.38.refs_0_), channel_id=1, source_target_pairs={{0,24},{8,0},{16,8},{24,16},{1,25},{9,1},{17,9},{25,17},{2,26},{10... | collective-permute-start | bytes 393224 | tf_op jit(solution)/shard_map/ppermute | solution.py:218
  14.6 5.4 %collective-permute-start = (bf16[1,4,128,128]{3,2,1,0:T(8,128)(2,1)S(1)}, bf16[1,4,128,128]{3,2,1,0:T(8,128)(2,1)S(1)}, u32[]{:S(2)}, u32[]{:S(2)}) collective-permute-start(bf16[1,4,128,128]{3,2,1,0:T(8,128)(2,1)S(1)} %shard_map.38.refs_0_), channel_id=1, source_target_pairs={{0,8},{8,16},{16,24},{24,0},{1,9},{9,17},{17,25},{25,1},{2,10},{10... | collective-permute-start | bytes 393224 | tf_op jit(solution)/shard_map/ppermute | solution.py:218
  15.5 16.1 %all-to-all-start.1 = ((bf16[8,16,16,128]{3,2,1,0:T(8,128)(2,1)}), bf16[8,16,16,128]{3,2,1,0:T(8,128)(2,1)S(1)}, u32[]{:S(2)}, u32[]{:S(2)}) async-start(bf16[8,16,16,128]{3,2,1,0:T(8,128)(2,1)} %shard_map.40), calls=%async_computation.1 | async-start | bytes 1048576 | tf_op jit(solution)/shard_map/all_to_all | solution.py:269
  20.6 23.2 %copy-start.2 = (s32[4]{0:T(128)S(1)}, s32[4]{0:T(128)}, u32[]{:S(2)}) copy-start(s32[4]{0:T(128)} %docs_ref.9) | copy-start | bytes 52
  20.6 12.2 %collective-permute-start.3 = (bf16[3,4,128,128]{3,2,1,0:T(8,128)(2,1)S(1)}, bf16[3,4,128,128]{3,2,1,0:T(8,128)(2,1)S(1)}, u32[]{:S(2)}, u32[]{:S(2)}) collective-permute-start(bf16[3,4,128,128]{3,2,1,0:T(8,128)(2,1)S(1)} %shard_map.39.refs_0_), channel_id=1, source_target_pairs={{0,224},{32,0},{64,32},{96,64},{128,96},{160,128},{192,160},{224,1... | collective-permute-start | bytes 1179656 | tf_op jit(solution)/shard_map/ppermute | solution.py:218
  26.3 9.7 %collective-permute-start.2 = (bf16[3,4,128,128]{3,2,1,0:T(8,128)(2,1)S(1)}, bf16[3,4,128,128]{3,2,1,0:T(8,128)(2,1)S(1)}, u32[]{:S(2)}, u32[]{:S(2)}) collective-permute-start(bf16[3,4,128,128]{3,2,1,0:T(8,128)(2,1)S(1)} %shard_map.39.refs_0_), channel_id=1, source_target_pairs={{0,32},{32,64},{64,96},{96,128},{128,160},{160,192},{192,224},{224... | collective-permute-start | bytes 1179656 | tf_op jit(solution)/shard_map/ppermute | solution.py:218
  26.3 5.3 %collective-permute-start.4 = (bf16[1,4,128,128]{3,2,1,0:T(8,128)(2,1)S(1)}, bf16[1,4,128,128]{3,2,1,0:T(8,128)(2,1)S(1)}, u32[]{:S(2)}, u32[]{:S(2)}) collective-permute-start(bf16[1,4,128,128]{3,2,1,0:T(8,128)(2,1)S(1)} %shard_map.38.refs_0_), channel_id=1, source_target_pairs={{0,16},{8,24},{16,0},{24,8},{1,17},{9,25},{17,1},{25,9},{2,18},{10... | collective-permute-start | bytes 393224 | tf_op jit(solution)/shard_map/ppermute | solution.py:218
  35.9 10.8 %collective-permute-start.5 = (bf16[3,4,128,128]{3,2,1,0:T(8,128)(2,1)S(1)}, bf16[3,4,128,128]{3,2,1,0:T(8,128)(2,1)S(1)}, u32[]{:S(2)}, u32[]{:S(2)}) collective-permute-start(bf16[3,4,128,128]{3,2,1,0:T(8,128)(2,1)S(1)} %collective-permute-done.2.refs_0_), channel_id=1, source_target_pairs={{0,32},{32,64},{64,96},{96,128},{128,160},{160,192},{192,224},{224... | collective-permute-start | bytes 1179656 | tf_op jit(solution)/shard_map/ppermute | solution.py:218
  35.9 10.8 %collective-permute-start.6 = (bf16[3,4,128,128]{3,2,1,0:T(8,128)(2,1)S(1)}, bf16[3,4,128,128]{3,2,1,0:T(8,128)(2,1)S(1)}, u32[]{:S(2)}, u32[]{:S(2)}) collective-permute-start(bf16[3,4,128,128]{3,2,1,0:T(8,128)(2,1)S(1)} %collective-permute-done.3.refs_1_), channel_id=1, source_target_pairs={{0,224},{32,0},{64,32},{96,64},{128,96},{160,128},{192,160},{224,1... | collective-permute-start | bytes 1179656 | tf_op jit(solution)/shard_map/ppermute | solution.py:218
  39.0 15.6 %collective-permute-start.9 = (bf16[2,4,128,128]{3,2,1,0:T(8,128)(2,1)S(1)}, bf16[2,4,128,128]{3,2,1,0:T(8,128)(2,1)S(1)}, u32[]{:S(2)}, u32[]{:S(2)}) collective-permute-start(bf16[2,4,128,128]{3,2,1,0:T(8,128)(2,1)S(1)} %shard_map.42), channel_id=1, source_target_pairs={{0,24},{8,0},{16,8},{24,16},{1,25},{9,1},{17,9},{25,17},{2,26},{10... | collective-permute-start | bytes 786440 | tf_op jit(solution)/shard_map/ppermute | solution.py:218
  46.8 9.8 %collective-permute-start.7 = (bf16[3,4,128,128]{3,2,1,0:T(8,128)(2,1)S(1)}, bf16[3,4,128,128]{3,2,1,0:T(8,128)(2,1)S(1)}, u32[]{:S(2)}, u32[]{:S(2)}) collective-permute-start(bf16[3,4,128,128]{3,2,1,0:T(8,128)(2,1)S(1)} %collective-permute-done.5.refs_0_), channel_id=1, source_target_pairs={{0,32},{32,64},{64,96},{96,128},{128,160},{160,192},{192,224},{224... | collective-permute-start | bytes 1179656 | tf_op jit(solution)/shard_map/ppermute | solution.py:218
  46.8 9.7 %collective-permute-start.8 = (bf16[3,4,128,128]{3,2,1,0:T(8,128)(2,1)S(1)}, bf16[3,4,128,128]{3,2,1,0:T(8,128)(2,1)S(1)}, u32[]{:S(2)}, u32[]{:S(2)}) collective-permute-start(bf16[3,4,128,128]{3,2,1,0:T(8,128)(2,1)S(1)} %collective-permute-done.6.refs_1_), channel_id=1, source_target_pairs={{0,224},{32,0},{64,32},{96,64},{128,96},{160,128},{192,160},{224,1... | collective-permute-start | bytes 1179656 | tf_op jit(solution)/shard_map/ppermute | solution.py:218
  49.8 14.3 %collective-permute-start.12 = (bf16[2,4,128,128]{3,2,1,0:T(8,128)(2,1)S(1)}, bf16[2,4,128,128]{3,2,1,0:T(8,128)(2,1)S(1)}, u32[]{:S(2)}, u32[]{:S(2)}) collective-permute-start(bf16[2,4,128,128]{3,2,1,0:T(8,128)(2,1)S(1)} %shard_map.45), channel_id=1, source_target_pairs={{0,24},{8,0},{16,8},{24,16},{1,25},{9,1},{17,9},{25,17},{2,26},{10... | collective-permute-start | bytes 786440 | tf_op jit(solution)/shard_map/ppermute | solution.py:218
  57.1 9.0 %collective-permute-start.10 = (bf16[2,4,128,128]{3,2,1,0:T(8,128)(2,1)S(1)}, bf16[2,4,128,128]{3,2,1,0:T(8,128)(2,1)S(1)}, u32[]{:S(2)}, u32[]{:S(2)}) collective-permute-start(bf16[2,4,128,128]{3,2,1,0:T(8,128)(2,1)S(1)} %get-tuple-element.62), channel_id=1, source_target_pairs={{0,32},{32,64},{64,96},{96,128},{128,160},{160,192},{192,224},{224... | collective-permute-start | bytes 786440 | tf_op jit(solution)/shard_map/ppermute | solution.py:218
  57.2 10.7 %collective-permute-start.14 = (bf16[2,4,128,128]{3,2,1,0:T(8,128)(2,1)S(1)}, bf16[2,4,128,128]{3,2,1,0:T(8,128)(2,1)S(1)}, u32[]{:S(2)}, u32[]{:S(2)}) collective-permute-start(bf16[2,4,128,128]{3,2,1,0:T(8,128)(2,1)S(1)} %get-tuple-element.72), channel_id=1, source_target_pairs={{0,24},{8,0},{16,8},{24,16},{1,25},{9,1},{17,9},{25,17},{2,26},{10... | collective-permute-start | bytes 786440 | tf_op jit(solution)/shard_map/ppermute | solution.py:218
  61.6 4.5 %collective-permute-start.11 = (bf16[1,4,128,128]{3,2,1,0:T(8,128)(2,1)S(1)}, bf16[1,4,128,128]{3,2,1,0:T(8,128)(2,1)S(1)}, u32[]{:S(2)}, u32[]{:S(2)}) collective-permute-start(bf16[1,4,128,128]{3,2,1,0:T(8,128)(2,1)S(1)} %get-tuple-element.63), channel_id=1, source_target_pairs={{0,224},{32,0},{64,32},{96,64},{128,96},{160,128},{192,160},{224,1... | collective-permute-start | bytes 393224 | tf_op jit(solution)/shard_map/ppermute | solution.py:218
  66.1 3.9 %collective-permute-start.13 = (bf16[1,4,128,128]{3,2,1,0:T(8,128)(2,1)S(1)}, bf16[1,4,128,128]{3,2,1,0:T(8,128)(2,1)S(1)}, u32[]{:S(2)}, u32[]{:S(2)}) collective-permute-start(bf16[1,4,128,128]{3,2,1,0:T(8,128)(2,1)S(1)} %collective-permute-done.11.refs_1_), channel_id=1, source_target_pairs={{0,24},{8,0},{16,8},{24,16},{1,25},{9,1},{17,9},{25,17},{2,26},{10... | collective-permute-start | bytes 393224 | tf_op jit(solution)/shard_map/ppermute | solution.py:218
  71.4 6.9 %collective-permute-start.15 = (bf16[4,2,16,1024]{3,2,1,0:T(8,128)(2,1)S(1)}, bf16[4,2,16,1024]{3,2,1,0:T(8,128)(2,1)S(1)}, u32[]{:S(2)}, u32[]{:S(2)}) collective-permute-start(bf16[4,2,16,1024]{3,2,1,0:T(8,128)(2,1)S(1)} %shard_map.49), channel_id=1, source_target_pairs={{0,1},{1,0},{2,3},{3,2},{4,5},{5,4},{6,7},{7,6},{8,9},{9,8},{10,11... | collective-permute-start | bytes 786440 | tf_op jit(solution)/shard_map/ppermute | solution.py:233
  78.8 6.0 %collective-permute-start.16 = (bf16[2,2,16,1024]{3,2,1,0:T(8,128)(2,1)S(1)}, bf16[2,2,16,1024]{3,2,1,0:T(8,128)(2,1)S(1)}, u32[]{:S(2)}, u32[]{:S(2)}) collective-permute-start(bf16[2,2,16,1024]{3,2,1,0:T(8,128)(2,1)S(1)} %get-tuple-element.80), channel_id=1, source_target_pairs={{0,2},{1,3},{2,4},{3,5},{4,6},{5,7},{6,0},{7,1},{8,10},{9,11},{10,... | collective-permute-start | bytes 393224 | tf_op jit(solution)/shard_map/ppermute | solution.py:244
  79.8 8.5 %collective-permute-start.17 = (bf16[2,2,16,1024]{3,2,1,0:T(8,128)(2,1)S(1)}, bf16[2,2,16,1024]{3,2,1,0:T(8,128)(2,1)S(1)}, u32[]{:S(2)}, u32[]{:S(2)}) collective-permute-start(bf16[2,2,16,1024]{3,2,1,0:T(8,128)(2,1)S(1)} %get-tuple-element.81), channel_id=1, source_target_pairs={{0,4},{1,5},{2,6},{3,7},{4,0},{5,1},{6,2},{7,3},{8,12},{9,13},{10,... | collective-permute-start | bytes 393224 | tf_op jit(solution)/shard_map/ppermute | solution.py:244
  82.2 6.1 %collective-permute-start.18 = (bf16[2,2,16,1024]{3,2,1,0:T(8,128)(2,1)S(1)}, bf16[2,2,16,1024]{3,2,1,0:T(8,128)(2,1)S(1)}, u32[]{:S(2)}, u32[]{:S(2)}) collective-permute-start(bf16[2,2,16,1024]{3,2,1,0:T(8,128)(2,1)S(1)} %get-tuple-element.82), channel_id=1, source_target_pairs={{0,6},{1,7},{2,0},{3,1},{4,2},{5,3},{6,4},{7,5},{8,14},{9,15},{10,... | collective-permute-start | bytes 393224 | tf_op jit(solution)/shard_map/ppermute | solution.py:244
